TPU v7x, 32 devices: a whole 2x2x4 slice. The times are simulated.
32 devices in a mesh: col: 16 (over z, y, x), row: 2 (over core).
Axes of the slice: x: 2, y: 2, z: 4, core: 2. Of those that a mesh axis runs over, the one named last changes fastest.
Arguments:
- x_block: bfloat16 [2, 2048, 64], P('row', 'col'), may hold values from -6 to 6
- tiles: bfloat16 [16, 2, 96, 128, 128], P('col', 'row'), may hold values from -0.078125 to 0.078125
- tile_rows: int32 [16, 2, 96], P('col', 'row'), may hold values from 0 to 15
- tile_cols: int32 [16, 2, 96], P('col', 'row'), may hold values from 0 to 1
- tile_count: int32 [16, 2], P('col', 'row'), may hold values from 1 to 96, as said below
Outputs:
- filtered: bfloat16 [2, 2048, 64], P('row', 'col')
- gram: float32 [64, 64], replicated
Inputs may be any that keep to these rules, and one draw needn't show every extreme that they name: `tile_count`: padding slots hold arbitrary tiles and indices; every draw has some device with all 96 slots live.
All inputs are finite; a program needn't handle non-finite values.
Results may differ from a plain program's by a relative error of at most 0.0049.
Values may be sent and summed in bfloat16 or wider, within the bound.
No kernel may reach another device: no remote copies, remote signals or barrier semaphores. Data moves between devices by JAX's collectives and lax.ppermute only.
A program may use at most 64 MiB of HBM per device.

v0:
```python
import jax
import jax.numpy as jnp
from jax import lax
from jax.sharding import PartitionSpec as P


def local(x_block, tiles, tile_rows, tile_cols, tile_count):
    n_col = lax.axis_size("col")
    n_row = lax.axis_size("row")
    tile_data = tiles[0, 0]
    rows_here = tile_rows[0, 0]
    cols_here = tile_cols[0, 0]
    count_here = tile_count[0, 0]
    vectors = x_block.shape[2]
    slots = tile_data.shape[0]
    live = jnp.arange(slots, dtype=jnp.int32) < count_here
    placing = (
        (rows_here[None, :] == jnp.arange(n_col, dtype=jnp.int32)[:, None]) & live[None, :]
    ).astype(jnp.float32)

    def apply_local(segment):
        slab_vecs = lax.all_gather(segment[0], "row", axis=0, tiled=True)
        picked = slab_vecs.reshape(n_row, 128, vectors)[cols_here]
        products = jnp.einsum("tij,tjk->tik", tile_data, picked, preferred_element_type=jnp.float32)
        products = products.reshape(slots, 128 * vectors)
        band_sums = jnp.dot(placing, products, precision=lax.Precision.HIGH)
        owned = lax.psum_scatter(band_sums, "col", scatter_dimension=0, tiled=True)
        return owned.reshape(1, 128, vectors)

    first = apply_local(x_block).astype(jnp.bfloat16)
    second = apply_local(first)
    gram_term = jnp.dot(first[0].astype(jnp.float32).T, second[0], precision=lax.Precision.HIGHEST)
    gram = lax.psum(gram_term, ("col", "row")) / (n_col * n_row * 128)
    return (second.astype(jnp.bfloat16), gram)


def solution(mesh):
    placed = (
        P("row", "col", None),
        P("col", "row", None, None, None),
        P("col", "row", None),
        P("col", "row", None),
        P("col", "row"),
    )
    return jax.shard_map(
        local, mesh=mesh, in_specs=placed, out_specs=(P("row", "col", None), P()), check_vma=False
    )
```

profile of v0, /device:TPU:0, one launch (start us, length us, event | category | flops | bytes accessed | tf_op | source)
XLA Modules:
  0.0 288.8 jit_solution(7156462486837419224)
XLA Ops:
  7.2 0.0 copy-start
  7.2 0.0 all-reduce.5.cloned.1.call-start
  8.0 0.7 fusion.20
  8.8 2.2 all-gather
  11.1 2.0 gather_fusion
  13.0 0.0 copy-done
  13.0 5.3 %fusion.4 = f32[96,128,64]{1,2,0:T(8,128)} fusion(bf16[96,128,64]{1,2,0:T(8,128)(2,1)} %gather_fusion, bf16[1,1,96,128,128]{4,3,2,1,0:T(8,128)(2,1)S(1)} %copy-done), kind=kOutput, calls=%fused_computation.6 | convolution fusion | flops 201326592 | bytes 7864320 | tf_op jit(solution)/shard_map/tij,tjk->tik/dot_general | solution.py:24
  18.4 0.0 copy-start.1
  18.4 5.1 %copy.18 = f32[96,128,64]{0,2,1:T(8,128)} copy(f32[96,128,64]{1,2,0:T(8,128)} %fusion.4) | data formatting | bytes 6291456 | tf_op jit(solution)/shard_map/tij,tjk->tik/dot_general | solution.py:24
  23.4 0.0 copy-start.2
  23.4 0.0 copy-done.1
  23.4 4.2 %fusion.14 = f32[16,8192]{1,0:T(8,128)} fusion(f32[96,8192]{0,1:T(8,128)} %bitcast.33, s32[96]{0:T(128)S(1)} %bitcast.35, pred[96]{0:T(512)(128)(4,1)S(1)} %iota_compare_fusion.1), kind=kOutput, calls=%fused_computation.16 | convolution fusion | flops 75500544 | bytes 3670496 | tf_op jit(solution)/shard_map/dot_general | solution.py:26
  27.6 85.0 %all-reduce.6 = bf16[16,8192]{1,0:T(8,128)(2,1)S(1)} all-reduce(f32[16,8192]{1,0:T(8,128)} %fusion.14), channel_id=3, replica_groups=mesh['col'=16,'row'=2] {'col'}, use_global_device_ids=true, to_apply=%region_0.0.clone | all-reduce | flops 131072 | bytes 786432
  112.7 0.0 copy-done.2
  112.7 0.6 dynamic-slice
  113.3 0.8 fusion.10
  114.0 0.1 convert_element_type.27
  114.1 1.8 all_gather.7
  115.9 0.1 copy.20
  116.0 2.0 gather_fusion.1
  118.0 5.3 %fusion.7 = f32[96,128,64]{1,2,0:T(8,128)} fusion(bf16[96,128,64]{1,2,0:T(8,128)(2,1)} %gather_fusion.1, bf16[1,1,96,128,128]{4,3,2,1,0:T(8,128)(2,1)S(1)} %copy-done), kind=kOutput, calls=%fused_computation.7 | convolution fusion | flops 201326592 | bytes 7864320 | tf_op jit(solution)/shard_map/tij,tjk->tik/dot_general | solution.py:24
  123.3 5.1 %copy.21 = f32[96,128,64]{0,2,1:T(8,128)} copy(f32[96,128,64]{1,2,0:T(8,128)} %fusion.7) | data formatting | bytes 6291456 | tf_op jit(solution)/shard_map/tij,tjk->tik/dot_general | solution.py:24
  128.4 4.2 %fusion.12 = f32[16,8192]{1,0:T(8,128)} fusion(f32[96,8192]{0,1:T(8,128)} %bitcast.32, s32[96]{0:T(128)S(1)} %bitcast.36, pred[96]{0:T(512)(128)(4,1)S(1)} %iota_compare_fusion.1), kind=kOutput, calls=%fused_computation.15 | convolution fusion | flops 75500544 | bytes 3670496 | tf_op jit(solution)/shard_map/dot_general | solution.py:26
  132.6 0.0 all-reduce.5.cloned.1.call-update
  132.6 104.8 %all-reduce.5.cloned.1.call-done = f32[16,8192]{1,0:T(8,128)} async-done(((f32[16,8192]{1,0:T(8,128)}), f32[16,8192]{1,0:T(8,128)}) %all-reduce.5.cloned.1.call-update) | async-done | bytes 524304
  237.4 1.7 convert_reduce_fusion
  239.1 0.1 convert_element_type.29
  239.1 0.7 copy.22
  239.8 1.7 dynamic-slice_reduce_fusion
  241.5 0.1 squeeze_reshape.3
  241.6 0.2 fusion.21
  241.8 39.5 %psum.7 = f32[64,64]{1,0:T(8,128)S(1)} all-reduce(f32[64,64]{1,0:T(8,128)S(1)} %fusion.21), channel_id=1, replica_groups=mesh['col'=16,'row'=2] {'col','row'}, use_global_device_ids=true, to_apply=%region_2.0 | all-reduce | flops 4096 | bytes 32768 | tf_op jit(solution)/shard_map/psum | solution.py:33
  281.3 0.6 broadcast_multiply_fusion
  (4 shorter events, 0.0 us)
Async XLA Ops:
  7.2 5.9 %copy-start = (bf16[1,1,96,128,128]{4,3,2,1,0:T(8,128)(2,1)S(1)}, bf16[1,1,96,128,128]{4,3,2,1,0:T(8,128)(2,1)}, u32[]{:S(2)}) copy-start(bf16[1,1,96,128,128]{4,3,2,1,0:T(8,128)(2,1)} %param.6) | copy-start | bytes 9437188
  7.2 230.2 %all-reduce.5.cloned.1.call-start = ((), (), s32[]{:S(2)}) async-start(), calls=%async_computation | async-start | bytes 1048576
  18.4 5.1 %copy-start.1 = (s32[1,1,96]{2,1,0:T(1,128)S(1)}, s32[1,1,96]{2,1,0:T(1,128)}, u32[]{:S(2)}) copy-start(s32[1,1,96]{2,1,0:T(1,128)} %param.7) | copy-start | bytes 1156
  23.4 89.2 %copy-start.2 = (u32[32]{0:T(128)S(1)}, u32[32]{0:T(128)}, u32[]{:S(2)}) copy-start(u32[32]{0:T(128)} %constant.14) | copy-start | bytes 388
Sparse Core Ops, SparseCore 0:
  132.7 104.5 all-reduce.4
where the time goes:
time: 289 us
  blocking collectives  129 us (45%)
  waiting for transfers between devices  105 us (36%)
  local copies, waits for them, and re-layouts  19.8 us (7%)
  matrix products  19.3 us (7%)
  between operations  14.9 us (5%)
    unnamed x2, waiting for transfers between devices  105 us
    unnamed x1, blocking collectives  85 us
    psum x1, blocking collectives, local(): gram = lax.psum(gram_term, ('col', 'row')) / (n_col * n_row * 128)  39.5 us
    dot_general x2, matrix products, apply_local(): jnp.einsum('tij,tjk->tik', tile_data, picked, preferred_element_type=jnp....  10.7 us
    dot_general x2, local copies, waits for them, and re-layouts, apply_local(): jnp.einsum('tij,tjk->tik', tile_data, picked, preferred_element_type=jnp....  10.1 us
    dot_general x2, matrix products, apply_local(): band_sums = jnp.dot(placing, products, precision=lax.Precision.HIGH)  8.38 us
  transfers between devices with their start and end apart: 1, of which 1 were waited for; matrix products, arithmetic and copies ran while one was open for 0% of the time, Pallas kernels for 0%

commit v1 on v0

v1 whole, which is shorter than its diff:
```python
import functools

import jax
import jax.numpy as jnp
from jax import lax
from jax.experimental import pallas as pl
from jax.experimental.pallas import tpu as pltpu
from jax.sharding import PartitionSpec as P

F32 = jnp.float32
BF16 = jnp.bfloat16
MIB = 1 << 20


def lane_half(shape):
    return lax.broadcasted_iota(jnp.int32, shape, len(shape) - 1) // 64


def swap_halves(value):
    return pltpu.roll(value, 64, 1)


def pack(block):
    top, low = block[:64], block[64:]
    return jnp.where(lane_half(top.shape) == 0, top, swap_halves(low))


def apply_kernel(
    n_col, n_row, slots, group, rows_ref, cols_ref, count_ref, vecs_ref, tiles_ref, out_ref, staged, right, products, total, sems
):
    chunks = slots // group
    copies = [
        pltpu.make_async_copy(tiles_ref.at[0, 0, pl.ds(i * group, group)], staged.at[pl.ds(i * group, group)], sems.at[i])
        for i in range(chunks)
    ]
    for copy in copies:
        copy.start()
    lane_groups = n_row // 2
    packed = vecs_ref.shape[1] == 64
    right[...] = jnp.zeros_like(right)
    for g in range(lane_groups):
        even, odd = vecs_ref[2 * g].astype(F32), vecs_ref[2 * g + 1].astype(F32)
        if packed:
            low = lane_half(even.shape) == 0
            upper = jnp.where(low, even, swap_halves(odd))
            lower = jnp.where(low, swap_halves(even), odd)
            both = jnp.concatenate([upper, lower], axis=0)
        else:
            both = jnp.concatenate([even, odd], axis=1)
        both = both.astype(BF16)
        right[g, :128, :128] = both
        right[g, 128:, 128:] = both
    total[...] = jnp.zeros_like(total)
    half = lane_half((128, 128))
    count = count_ref[0, 0]
    for i in range(chunks):
        copies[i].wait()
        pairs = staged[pl.ds(i * group, group)].reshape(group // 2, 2, 128, 128)
        left = jnp.concatenate([pairs[:, 0], pairs[:, 1]], axis=-1).reshape(group * 64, 256)
        for g in range(lane_groups):
            products[g] = jnp.dot(left, right[g], preferred_element_type=F32)
        for j in range(group):
            slot = i * group + j
            band = cols_ref[0, 0, slot]
            place = jnp.clip(rows_ref[0, 0, slot], 0, n_col - 1)
            lane_group = jnp.clip(band // 2, 0, lane_groups - 1) if lane_groups > 1 else 0
            wanted = jnp.where(slot < count, band % 2, 2)
            term = products[lane_group, pl.ds(j // 2 * 128, 128), pl.ds(j % 2 * 128, 128)]
            total[place] += jnp.where(half == wanted, term, 0.0)
    for r in range(n_col):
        block = total[r]
        out_ref[r] = pack(block + swap_halves(block)).astype(BF16)


def apply_local(tiles, rows, cols, count, vecs, n_col):
    n_row, slots = vecs.shape[0], tiles.shape[2]
    group = next(g for g in (16, 8, 4, 2) if slots % g == 0)
    smem = pl.BlockSpec(memory_space=pltpu.SMEM)
    vmem = pl.BlockSpec(memory_space=pltpu.VMEM)
    return pl.pallas_call(
        functools.partial(apply_kernel, n_col, n_row, slots, group),
        out_shape=jax.ShapeDtypeStruct((n_col, 64, 128), BF16),
        in_specs=[smem, smem, smem, vmem, pl.BlockSpec(memory_space=pl.ANY)],
        out_specs=vmem,
        scratch_shapes=[
            pltpu.VMEM((slots, 128, 128), BF16),
            pltpu.VMEM((n_row // 2, 256, 256), BF16),
            pltpu.VMEM((n_row // 2, group * 64, 256), F32),
            pltpu.VMEM((n_col, 128, 128), F32),
            pltpu.SemaphoreType.DMA((slots // group,)),
        ],
        compiler_params=pltpu.CompilerParams(vmem_limit_bytes=32 * MIB),
        cost_estimate=pl.CostEstimate(flops=slots * 128 * 128 * 128, bytes_accessed=slots * 128 * 256, transcendentals=0),
        name="tile_products",
    )(rows, cols, count, vecs, tiles)


def sum_kernel(parts_ref, out_ref):
    out_ref[...] = jnp.sum(parts_ref[...].astype(F32), axis=0).astype(BF16)


def sum_parts(parts):
    return pl.pallas_call(
        sum_kernel, out_shape=jax.ShapeDtypeStruct(parts.shape[1:], BF16), name="sum_parts"
    )(parts)


def gram_kernel(copies, parts_ref, first_ref, filtered_ref, terms_ref):
    second = jnp.sum(parts_ref[...].astype(F32), axis=0)
    filtered_ref[0, :64, :] = second[:, :64].astype(BF16)
    filtered_ref[0, 64:, :] = swap_halves(second)[:, :64].astype(BF16)
    first = first_ref[...]
    high = second.astype(BF16)
    low = (second - high.astype(F32)).astype(BF16)
    dims = (((0,), (0,)), ((), ()))
    full = lax.dot_general(first, high, dims, preferred_element_type=F32)
    full += lax.dot_general(first, low, dims, preferred_element_type=F32)
    term = full[:64] + swap_halves(full[64:])
    term = jnp.where(lane_half((32, 128)) == 0, term[:32], swap_halves(term[32:])).astype(BF16)
    for i in range(copies):
        terms_ref[i] = term


def gram_term(parts, first, copies):
    return pl.pallas_call(
        functools.partial(gram_kernel, copies),
        out_shape=(
            jax.ShapeDtypeStruct((1, 128, 64), BF16),
            jax.ShapeDtypeStruct((copies, 32, 128), BF16),
        ),
        name="gram_term",
    )(parts, first)


def gram_sum_kernel(scale, terms_ref, out_ref):
    total = jnp.sum(terms_ref[...].astype(F32), axis=0) * scale
    out_ref[:32] = total[:, :64]
    out_ref[32:] = swap_halves(total)[:, :64]


def gram_sum(terms, scale):
    return pl.pallas_call(
        functools.partial(gram_sum_kernel, scale), out_shape=jax.ShapeDtypeStruct((64, 64), F32), name="gram_sum"
    )(terms)


def local(x_block, tiles, tile_rows, tile_cols, tile_count):
    n_col = lax.axis_size("col")
    n_row = lax.axis_size("row")

    def apply_owned(vecs):
        bands = lax.all_gather(vecs, "row", axis=0, tiled=True)
        partial = apply_local(tiles, tile_rows, tile_cols, tile_count, bands, n_col)
        return lax.all_to_all(partial, "col", 0, 0, tiled=True)

    first = sum_parts(apply_owned(x_block))
    filtered, terms = gram_term(apply_owned(first[None]), first, n_col * n_row)
    terms = lax.all_to_all(terms, ("col", "row"), 0, 0, tiled=True)
    return filtered, gram_sum(terms, 1.0 / (n_col * n_row * 128))


def solution(mesh):
    placed = (
        P("row", "col", None),
        P("col", "row", None, None, None),
        P("col", "row", None),
        P("col", "row", None),
        P("col", "row"),
    )
    return jax.shard_map(
        local, mesh=mesh, in_specs=placed, out_specs=(P("row", "col", None), P()), check_vma=False
    )
```

time: 289 us -> 68.3 us (0.24)
  waiting for transfers between devices: 105 us -> 9.15 us
  blocking collectives: 129 us -> 36.2 us
  matrix products: 19.3 us -> 0 us
  local copies, waits for them, and re-layouts: 19.8 us -> 5.48 us
  between operations: 14.9 us -> 1.36 us
  Pallas kernels: 0 us -> 13 us
    unnamed x2 -> x0, waiting for transfers between devices: 105 us -> none
    unnamed x1 -> x0, blocking collectives: 85 us -> none
    psum x1 -> x0, blocking collectives: 39.5 us -> none  [local(): gram = lax.psum(gram_term, ('col', 'row')) / (n_col * n_row * 128)]
    all_to_all x0 -> x2, blocking collectives: none -> 32 us  [apply_owned(): return lax.all_to_all(partial, 'col', 0, 0, tiled=True)]
    dot_general x5 -> x0, matrix products: 19.3 us -> none  [the longest x2 10.7 us: apply_local(): jnp.einsum('tij,tjk->tik', tile_data, picked, preferred_element_type=jnp....]
    pallas_call x0 -> x5, Pallas kernels: none -> 13 us  [the longest x2 7.76 us: apply_local(): pl.pallas_call(functools.partial(apply_kernel, n_col, n_row, slots, group...]
    dot_general x2 -> x0, local copies, waits for them, and re-layouts: 10.1 us -> none  [apply_local(): jnp.einsum('tij,tjk->tik', tile_data, picked, preferred_element_type=jnp....]
    all_to_all x0 -> x1, waiting for transfers between devices: none -> 9.15 us  [local(): terms = lax.all_to_all(terms, ('col', 'row'), 0, 0, tiled=True)]
  transfers between devices with their start and end apart: 1 -> 1, of which waited for: 1 -> 1; matrix products, arithmetic and copies ran while one was open for 0% -> 2% of each run, Pallas kernels for 0% -> 0%
where the time goes in v1:
time: 68.3 us; the launch traced here: 67.9 us
  blocking collectives  36.2 us (53%)
  Pallas kernels  13 us (19%)
  waiting for transfers between devices  9.15 us (13%)
  local copies, waits for them, and re-layouts  5.48 us (8%)
  starting transfers between devices  2.58 us (4%)
  between operations  1.36 us (2%)
    all_to_all x2, blocking collectives, apply_owned(): return lax.all_to_all(partial, 'col', 0, 0, tiled=True)  32 us
    all_to_all x1, waiting for transfers between devices, local(): terms = lax.all_to_all(terms, ('col', 'row'), 0, 0, tiled=True)  9.15 us
    pallas_call x2, Pallas kernels, apply_local(): pl.pallas_call(functools.partial(apply_kernel, n_col, n_row, slots, group...  7.76 us
    unnamed x15, local copies, waits for them, and re-layouts  5.36 us
    all_gather x2, blocking collectives, apply_owned(): bands = lax.all_gather(vecs, 'row', axis=0, tiled=True)  4.19 us
    all_to_all x1, starting transfers between devices, local(): terms = lax.all_to_all(terms, ('col', 'row'), 0, 0, tiled=True)  2.58 us
    pallas_call x1, Pallas kernels, gram_term(): pl.pallas_call(functools.partial(gram_kernel, copies), out_shape=(jax.Sha...  2.01 us
    pallas_call x1, Pallas kernels, gram_sum(): pl.pallas_call(functools.partial(gram_sum_kernel, scale), out_shape=jax.S...  1.69 us
  transfers between devices with their start and end apart: 1, of which 1 were waited for; matrix products, arithmetic and copies ran while one was open for 2% of the time, Pallas kernels for 0%

profile of v1, /device:TPU:0, one launch (start us, length us, event | category | flops | bytes accessed | tf_op | source)
XLA Modules:
  0.0 67.9 jit_solution(4637107220563867629)
XLA Ops:
  0.6 0.0 copy-start.5
  0.6 0.0 copy-start.3
  1.3 2.2 %all_gather.6 = bf16[2,128,64]{1,2,0:T(8,128)(2,1)S(1)} all-gather(bf16[1,128,64]{1,2,0:T(8,128)(2,1)} %param.5), channel_id=1, replica_groups=mesh['col'=16,'row'=2] {'row'}, dimensions={0}, use_global_device_ids=true | all-gather | bytes 49152 | tf_op jit(solution)/shard_map/all_gather | solution.py:152
  3.5 0.1 copy.9.vecs_ref
  3.6 0.0 copy-start
  3.6 1.9 %copy-done = bf16[1,1,96,128,128]{4,3,2,1,0:T(8,128)(2,1)S(1)} copy-done((bf16[1,1,96,128,128]{4,3,2,1,0:T(8,128)(2,1)S(1)}, bf16[1,1,96,128,128]{4,3,2,1,0:T(8,128)(2,1)}, u32[]{:S(2)}) %copy-start) | copy-done | bytes 3145752
  5.5 0.0 copy-start.2
  5.5 0.7 copy-done.2
  6.1 0.0 copy-start.4
  6.2 0.7 copy-done.4
  6.8 0.0 copy-start.1
  6.8 3.9 %tile_products.2 = bf16[16,64,128]{2,1,0:T(8,128)(2,1)S(1)} custom-call(s32[1,1,96]{2,1,0:T(1,128)S(1)} %copy-done.2, s32[1,1,96]{2,1,0:T(1,128)S(1)} %copy-done.4, s32[1,1]{1,0:T(1,128)S(6)} %copy.11.count_ref, bf16[2,128,64]{2,1,0:T(8,128)(2,1)S(1)} %copy.9.vecs_ref, bf16[1,1,96,128,128]{4,3,2,1,0:T(8,128)(2,1)S(1)} %copy-done), custom_call_target="tpu_custom_call" | custom-call | flops 201326592 | bytes 3145728 | tf_op jit(solution)/shard_map/tile_products/pallas_call | solution.py:80
  10.7 18.3 %all_to_all.15.parts_ref = bf16[16,64,128]{2,1,0:T(8,128)(2,1)} all-to-all(bf16[16,64,128]{2,1,0:T(8,128)(2,1)S(1)} %tile_products.2), channel_id=1, replica_groups=mesh['col'=16,'row'=2] {'col'}, dimensions={0} | all-to-all | bytes 524288 | tf_op jit(solution)/shard_map/all_to_all | solution.py:154
  29.0 1.6 %sum_parts.1.first_ref = bf16[64,128]{1,0:T(8,128)(2,1)} custom-call(bf16[16,64,128]{2,1,0:T(8,128)(2,1)} %all_to_all.15.parts_ref), custom_call_target="tpu_custom_call" | custom-call | tf_op jit(solution)/shard_map/sum_parts/pallas_call | solution.py:103
  30.6 2.0 %all-gather = bf16[128,128]{1,0:T(8,128)(2,1)S(1)} all-gather(bf16[64,128]{1,0:T(8,128)(2,1)} %sum_parts.1.first_ref), channel_id=2, replica_groups=mesh['col'=16,'row'=2] {'row'}, dimensions={0}, use_global_device_ids=true | all-gather | bytes 49152 | tf_op jit(solution)/shard_map/all_gather | solution.py:152
  32.6 0.0 copy-done.5
  32.6 0.0 copy-done.3
  32.6 0.0 copy-done.1
  32.6 3.9 %tile_products.3 = bf16[16,64,128]{2,1,0:T(8,128)(2,1)S(1)} custom-call(s32[1,1,96]{2,1,0:T(1,128)S(1)} %copy-done.3, s32[1,1,96]{2,1,0:T(1,128)S(1)} %copy-done.5, s32[1,1]{1,0:T(1,128)S(6)} %copy.11.count_ref, bf16[2,64,128]{2,1,0:T(8,128)(2,1)S(1)} %bitcast.1, bf16[1,1,96,128,128]{4,3,2,1,0:T(8,128)(2,1)S(1)} %copy-done.1), custom_call_target="tpu_custom_call" | custom-call | flops 201326592 | bytes 3145728 | tf_op jit(solution)/shard_map/tile_products/pallas_call | solution.py:80
  36.5 13.7 %all_to_all.16.parts_ref = bf16[16,64,128]{2,1,0:T(8,128)(2,1)} all-to-all(bf16[16,64,128]{2,1,0:T(8,128)(2,1)S(1)} %tile_products.3), channel_id=1, replica_groups=mesh['col'=16,'row'=2] {'col'}, dimensions={0} | all-to-all | bytes 524288 | tf_op jit(solution)/shard_map/all_to_all | solution.py:154
  50.3 2.0 %gram_term.1 = (bf16[1,128,64]{2,1,0:T(8,128)(2,1)}, bf16[32,32,128]{2,1,0:T(8,128)(2,1)}) custom-call(bf16[16,64,128]{2,1,0:T(8,128)(2,1)} %all_to_all.16.parts_ref, bf16[64,128]{1,0:T(8,128)(2,1)} %sum_parts.1.first_ref), custom_call_target="tpu_custom_call" | custom-call | tf_op jit(solution)/shard_map/gram_term/pallas_call | solution.py:125
  52.3 2.6 %all-to-all-start.2 = ((bf16[32,32,128]{2,1,0:T(8,128)(2,1)}), bf16[32,32,128]{2,1,0:T(8,128)(2,1)S(1)}, u32[]{:S(2)}, u32[]{:S(2)}) async-start(bf16[32,32,128]{2,1,0:T(8,128)(2,1)} %get-tuple-element.5), calls=%async_computation.2 | async-start | bytes 524288 | tf_op jit(solution)/shard_map/all_to_all | solution.py:158
  54.9 1.4 %copy.10 = bf16[1,128,64]{1,2,0:T(8,128)(2,1)} copy(bf16[1,128,64]{2,1,0:T(8,128)(2,1)} %get-tuple-element.8) | data formatting | bytes 32768
  56.3 9.1 %all-to-all-done.2.terms_ref = bf16[32,32,128]{2,1,0:T(8,128)(2,1)S(1)} async-done(((bf16[32,32,128]{2,1,0:T(8,128)(2,1)}), bf16[32,32,128]{2,1,0:T(8,128)(2,1)S(1)}, u32[]{:S(2)}, u32[]{:S(2)}) %all-to-all-start.2) | async-done | bytes 262176 | tf_op jit(solution)/shard_map/all_to_all | solution.py:158
  65.5 0.0 copy-start.6
  65.5 0.7 %copy-done.6 = bf16[32,32,128]{2,1,0:T(8,128)(2,1)} copy-done((bf16[32,32,128]{2,1,0:T(8,128)(2,1)}, bf16[32,32,128]{2,1,0:T(8,128)(2,1)S(1)}, u32[]{:S(2)}) %copy-start.6) | copy-done | bytes 262168
  66.2 1.7 %gram_sum.1 = f32[64,64]{1,0:T(8,128)} custom-call(bf16[32,32,128]{2,1,0:T(8,128)(2,1)} %copy-done.6), custom_call_target="tpu_custom_call" | custom-call | tf_op jit(solution)/shard_map/gram_sum/pallas_call | solution.py:142
Async XLA Ops:
  0.6 32.0 %copy-start.5 = (s32[1,1,96]{2,1,0:T(1,128)S(1)}, s32[1,1,96]{2,1,0:T(1,128)}, u32[]{:S(2)}) copy-start(s32[1,1,96]{2,1,0:T(1,128)} %cols_ref.3) | copy-start | bytes 1156
  0.6 32.0 %copy-start.3 = (s32[1,1,96]{2,1,0:T(1,128)S(1)}, s32[1,1,96]{2,1,0:T(1,128)}, u32[]{:S(2)}) copy-start(s32[1,1,96]{2,1,0:T(1,128)} %rows_ref.3) | copy-start | bytes 1156
  3.6 1.9 %copy-start = (bf16[1,1,96,128,128]{4,3,2,1,0:T(8,128)(2,1)S(1)}, bf16[1,1,96,128,128]{4,3,2,1,0:T(8,128)(2,1)}, u32[]{:S(2)}) copy-start(bf16[1,1,96,128,128]{4,3,2,1,0:T(8,128)(2,1)} %tiles_ref.3) | copy-start | bytes 9437188
  5.5 0.7 copy-start.2
  6.1 0.7 copy-start.4
  6.8 25.8 %copy-start.1 = (bf16[1,1,96,128,128]{4,3,2,1,0:T(8,128)(2,1)S(1)}, bf16[1,1,96,128,128]{4,3,2,1,0:T(8,128)(2,1)}, u32[]{:S(2)}) copy-start(bf16[1,1,96,128,128]{4,3,2,1,0:T(8,128)(2,1)} %tiles_ref.3) | copy-start | bytes 9437188
  52.3 13.2 %all-to-all-start.2 = ((bf16[32,32,128]{2,1,0:T(8,128)(2,1)}), bf16[32,32,128]{2,1,0:T(8,128)(2,1)S(1)}, u32[]{:S(2)}, u32[]{:S(2)}) async-start(bf16[32,32,128]{2,1,0:T(8,128)(2,1)} %get-tuple-element.5), calls=%async_computation.2 | async-start | bytes 524288 | tf_op jit(solution)/shard_map/all_to_all | solution.py:158
  65.5 0.7 %copy-start.6 = (bf16[32,32,128]{2,1,0:T(8,128)(2,1)}, bf16[32,32,128]{2,1,0:T(8,128)(2,1)S(1)}, u32[]{:S(2)}) copy-start(bf16[32,32,128]{2,1,0:T(8,128)(2,1)S(1)} %all-to-all-done.2.terms_ref) | copy-start | bytes 786436

commit v2 on v0

v2 whole, which is shorter than its diff:
```python
import functools
import math

import jax
import jax.numpy as jnp
from jax import lax
from jax.experimental import pallas as pl
from jax.experimental.pallas import tpu as pltpu
from jax.sharding import PartitionSpec as P

F32 = jnp.float32
BF16 = jnp.bfloat16
MIB = 1 << 20
SMEM = pl.BlockSpec(memory_space=pltpu.SMEM)
VMEM = pl.BlockSpec(memory_space=pltpu.VMEM)
ANY = pl.BlockSpec(memory_space=pl.ANY)


def low_lanes(shape):
    return lax.broadcasted_iota(jnp.int32, shape, len(shape) - 1) < 64


def swap_halves(value):
    return pltpu.roll(value, 64, 1)


def call(kernel, out_shape, in_specs, out_specs, scratch=(), mib=4, flops=0, size=0, **kwargs):
    return pl.pallas_call(
        kernel,
        out_shape=out_shape,
        in_specs=in_specs,
        out_specs=out_specs,
        scratch_shapes=list(scratch),
        compiler_params=pltpu.CompilerParams(vmem_limit_bytes=mib * MIB),
        cost_estimate=pl.CostEstimate(flops=flops, bytes_accessed=size, transcendentals=0),
        **kwargs,
    )


def stage_kernel(n_col, n_row, group, own_first, tiles_ref, rows_ref, cols_ref, count_ref, staged_ref, info_ref, rows, cols, count, sems):
    slots = staged_ref.shape[0]
    small = [
        pltpu.make_async_copy(source, target, sems.at[i])
        for i, (source, target) in enumerate(((rows_ref, rows), (cols_ref, cols), (count_ref, count)))
    ]
    large = [
        pltpu.make_async_copy(tiles_ref.at[0, 0, pl.ds(i * group, group)], staged_ref.at[pl.ds(i * group, group)], sems.at[3 + i])
        for i in range(slots // group)
    ]
    for copy in small + large:
        copy.start()
    for copy in small:
        copy.wait()
    slot = lax.broadcasted_iota(jnp.int32, (1, slots), 1)
    band = jnp.clip(cols[0], 0, n_row - 1)
    if own_first:
        band = lax.rem(band + n_row - lax.axis_index("row"), n_row)
    info_ref[0:1] = jnp.where(slot < count[...], jnp.clip(rows[0], 0, n_col - 1), n_col)
    info_ref[1:2] = band
    for copy in large:
        copy.wait()


def stage(tiles, rows, cols, count, n_col, n_row, own_first):
    slots = tiles.shape[2]
    group = math.gcd(slots, 16)
    tiles, rows, cols = (pltpu.with_memory_space_constraint(a, pltpu.HBM) for a in (tiles, rows, cols))
    return call(
        functools.partial(stage_kernel, n_col, n_row, group, own_first),
        (pltpu.VMEM((slots, 128, 128), BF16), jax.ShapeDtypeStruct((2, slots), jnp.int32)),
        [ANY] * 4,
        (VMEM, VMEM),
        [
            pltpu.VMEM(rows.shape, jnp.int32),
            pltpu.VMEM(cols.shape, jnp.int32),
            pltpu.VMEM(count.shape, jnp.int32),
            pltpu.SemaphoreType.DMA((3 + slots // group,)),
        ],
        mib=8,
        size=tiles.size * 2,
        name="stage_tiles",
    )(tiles, rows, cols, count)


def place_vectors(right, band, top, low):
    lanes = slice(band * 128, band * 128 + 128)
    mask = low_lanes(top.shape)
    for row, part in ((0, top), (64, low)):
        part = jnp.where(mask, part, 0.0)
        right[row : row + 64, lanes] = part.astype(BF16)
        right[128 + row : 192 + row, lanes] = swap_halves(part).astype(BF16)


def products_kernel(n_col, n_row, group, transposed, info_ref, tiles_ref, *refs):
    vecs, (out_ref, right, total) = refs[:-3], refs[-3:]
    slots = tiles_ref.shape[0]
    blocks = [ref[b].astype(F32) for ref in vecs for b in range(ref.shape[0])]
    for band, block in enumerate(blocks):
        if transposed:
            block = jnp.concatenate([block, jnp.zeros_like(block)], axis=0).T
            place_vectors(right, band, block[:64], block[64:])
        else:
            place_vectors(right, band, block, swap_halves(block))
    total[...] = jnp.zeros_like(total)
    for start in range(0, slots, group):
        pieces = tiles_ref[pl.ds(start, group)]
        left = jnp.concatenate([pieces[:, :64], pieces[:, 64:]], axis=-1).reshape(group * 64, 256)
        products = jnp.dot(left, right[...], preferred_element_type=F32)
        for j in range(group):
            band = info_ref[1, start + j]
            term = products[j * 64 : j * 64 + 64, :128]
            for b in range(1, n_row):
                term = jnp.where(band == b, products[j * 64 : j * 64 + 64, b * 128 : b * 128 + 128], term)
            total[info_ref[0, start + j]] += term
    out_ref[...] = total[:n_col].astype(BF16)


def tile_products(info, tiles, vecs, n_col, n_row, transposed):
    slots = tiles.shape[0]
    return call(
        functools.partial(products_kernel, n_col, n_row, math.gcd(slots, 4), transposed),
        jax.ShapeDtypeStruct((n_col, 64, 128), BF16),
        [SMEM] + [VMEM] * (1 + len(vecs)),
        VMEM,
        [pltpu.VMEM((256, n_row * 128), BF16), pltpu.VMEM((n_col + 1, 64, 128), F32)],
        mib=16,
        flops=slots * 64 * 256 * n_row * 256,
        size=slots * 128 * 256,
        name="tile_products",
    )(info, tiles, *vecs)


def sum_kernel(parts_ref, out_ref):
    out_ref[0] = jnp.sum(parts_ref[...].astype(F32), axis=0).astype(BF16)


def sum_parts(parts):
    shape = (1,) + parts.shape[1:]
    return call(sum_kernel, jax.ShapeDtypeStruct(shape, BF16), [VMEM], VMEM, size=parts.size * 2, name="sum_parts")(parts)


def gram_kernel(parts_ref, first_ref, filtered_ref, terms_ref):
    second = jnp.sum(parts_ref[...].astype(F32), axis=0)
    first = first_ref[0]
    high = second.astype(BF16)
    low = (second - high.astype(F32)).astype(BF16)
    dims = (((0,), (0,)), ((), ()))
    full = lax.dot_general(first, high, dims, preferred_element_type=F32)
    full += lax.dot_general(first, low, dims, preferred_element_type=F32)
    term = full[:64] + swap_halves(full[64:])
    term = jnp.where(low_lanes((32, 128)), term[:32], swap_halves(term[32:])).astype(BF16)
    terms_ref[...] = jnp.broadcast_to(term[None], terms_ref.shape)
    filtered_ref[0] = jnp.concatenate([second, swap_halves(second)], axis=0).T[:64].astype(BF16)


def gram_terms(parts, first, copies):
    return call(
        gram_kernel,
        (jax.ShapeDtypeStruct((1, 64, 128), BF16), jax.ShapeDtypeStruct((copies, 32, 128), BF16)),
        [VMEM, VMEM],
        (VMEM, VMEM),
        mib=8,
        size=parts.size * 2,
        name="gram_terms",
    )(parts, first)


def gram_sum_kernel(scale, terms_ref, out_ref):
    total = jnp.sum(terms_ref[...].astype(F32), axis=0) * scale
    out_ref[:32] = total[:, :64]
    out_ref[32:] = swap_halves(total)[:, :64]


def gram_sum(terms, scale):
    return call(
        functools.partial(gram_sum_kernel, scale),
        jax.ShapeDtypeStruct((64, 64), F32),
        [VMEM],
        VMEM,
        mib=8,
        size=terms.size * 2,
        name="gram_sum",
    )(terms)


def local(x_block, tiles, tile_rows, tile_cols, tile_count):
    n_col = lax.axis_size("col")
    n_row = lax.axis_size("row")
    pairs = n_row == 2

    def exchange(vecs):
        if pairs:
            return vecs, lax.ppermute(vecs, "row", [(0, 1), (1, 0)])
        return (lax.all_gather(vecs, "row", axis=0, tiled=True),)

    vecs = exchange(jnp.swapaxes(x_block, 1, 2))
    staged, info = stage(tiles, tile_rows, tile_cols, tile_count, n_col, n_row, pairs)
    partial = tile_products(info, staged, vecs, n_col, n_row, True)
    first = sum_parts(lax.all_to_all(partial, "col", 0, 0, tiled=True))
    partial = tile_products(info, staged, exchange(first), n_col, n_row, False)
    parts = lax.all_to_all(partial, "col", 0, 0, tiled=True)
    filtered, terms = gram_terms(parts, first, n_col * n_row)
    terms = lax.all_to_all(terms, ("col", "row"), 0, 0, tiled=True)
    return jnp.swapaxes(filtered, 1, 2), gram_sum(terms, 1.0 / (n_col * n_row * 128))


def solution(mesh):
    placed = (
        P("row", "col", None),
        P("col", "row", None, None, None),
        P("col", "row", None),
        P("col", "row", None),
        P("col", "row"),
    )
    return jax.shard_map(
        local, mesh=mesh, in_specs=placed, out_specs=(P("row", "col", None), P()), check_vma=False
    )
```

time: 289 us -> 55.4 us (0.19)
  waiting for transfers between devices: 105 us -> 1.17 us
  blocking collectives: 129 us -> 44.6 us
  local copies, waits for them, and re-layouts: 19.8 us -> 0.01 us
  matrix products: 19.3 us -> 0 us
  between operations: 14.9 us -> 1.34 us
  Pallas kernels: 0 us -> 7.39 us
    unnamed x2 -> x0, waiting for transfers between devices: 105 us -> none
    unnamed x1 -> x0, blocking collectives: 85 us -> none
    all_to_all x0 -> x3, blocking collectives: none -> 44.6 us  [the longest x1 18.2 us: local(): first = sum_parts(lax.all_to_all(partial, 'col', 0, 0, tiled=True))]
    psum x1 -> x0, blocking collectives: 39.5 us -> none  [local(): gram = lax.psum(gram_term, ('col', 'row')) / (n_col * n_row * 128)]
    dot_general x5 -> x0, matrix products: 19.3 us -> none  [the longest x2 10.7 us: apply_local(): jnp.einsum('tij,tjk->tik', tile_data, picked, preferred_element_type=jnp....]
    dot_general x2 -> x0, local copies, waits for them, and re-layouts: 10.1 us -> none  [apply_local(): jnp.einsum('tij,tjk->tik', tile_data, picked, preferred_element_type=jnp....]
    pallas_call x0 -> x6, Pallas kernels: none -> 7.39 us  [the longest x2 3.71 us: tile_products(): call(functools.partial(products_kernel, n_col, n_row, math.gcd(slots, 4),...]
    all_gather x2 -> x0, blocking collectives: 4.08 us -> none  [apply_local(): slab_vecs = lax.all_gather(segment[0], 'row', axis=0, tiled=True)]
  transfers between devices with their start and end apart: 1 -> 2, of which waited for: 1 -> 1; matrix products, arithmetic and copies ran while one was open for 0% -> 0% of each run, Pallas kernels for 0% -> 4%
where the time goes in v2:
time: 55.4 us; the launch traced here: 55.1 us
  blocking collectives  44.6 us (81%)
  Pallas kernels  7.39 us (13%)
  between operations  1.34 us (2%)
  waiting for transfers between devices  1.17 us (2%)
  starting transfers between devices  0.59 us (1%)
    all_to_all x1, blocking collectives, local(): first = sum_parts(lax.all_to_all(partial, 'col', 0, 0, tiled=True))  18.2 us
    all_to_all x1, blocking collectives, local(): parts = lax.all_to_all(partial, 'col', 0, 0, tiled=True)  13.5 us
    all_to_all x1, blocking collectives, local(): terms = lax.all_to_all(terms, ('col', 'row'), 0, 0, tiled=True)  12.9 us
    pallas_call x2, Pallas kernels, tile_products(): call(functools.partial(products_kernel, n_col, n_row, math.gcd(slots, 4),...  3.71 us
    pallas_call x1, Pallas kernels, stage(): call(functools.partial(stage_kernel, n_col, n_row, group, own_first), (pl...  1.94 us
    ppermute x2, waiting for transfers between devices, exchange(): return (vecs, lax.ppermute(vecs, 'row', [(0, 1), (1, 0)]))  1.17 us
  transfers between devices with their start and end apart: 2, of which 1 were waited for; matrix products, arithmetic and copies ran while one was open for 0% of the time, Pallas kernels for 4%

profile of v2, /device:TPU:0, one launch (start us, length us, event | category | flops | bytes accessed | tf_op | source)
XLA Modules:
  0.0 55.1 jit_solution(2025460162465327965)
XLA Ops:
  0.6 0.0 copy-start
  0.6 0.5 collective-permute-start
  1.8 1.9 %stage_tiles.1 = (bf16[96,128,128]{2,1,0:T(8,128)(2,1)S(1)}, s32[2,96]{1,0:T(2,128)S(1)}) custom-call(bf16[1,1,96,128,128]{4,3,2,1,0:T(8,128)(2,1)} %tiles_ref.1, s32[1,1,96]{2,1,0:T(1,128)} %rows_ref.1, s32[1,1,96]{2,1,0:T(1,128)} %cols_ref.1, s32[1,1]{1,0:T(1,128)S(6)} %copy.7.count_ref), custom_call_target="tpu_custom_call" | custom-call | bytes 3145728 | tf_op jit(solution)/shard_map/stage_tiles/pallas_call | solution.py:68
  3.8 0.0 collective-permute-done.refs_1_
  3.8 0.0 copy-done
  3.8 1.9 %tile_products.2 = bf16[16,64,128]{2,1,0:T(8,128)(2,1)S(1)} custom-call(s32[2,96]{1,0:T(2,128)S(1)} %get-tuple-element.6.info_ref, bf16[96,128,128]{2,1,0:T(8,128)(2,1)S(1)} %get-tuple-element.7.tiles_ref, bf16[1,64,128]{2,1,0:T(8,128)(2,1)S(1)} %bitcast.3, bf16[1,64,128]{2,1,0:T(8,128)(2,1)S(1)} %collective-permute-done.refs_1_), custom_call_target="tpu_custom_call" | custom-call | flops 805306368 | bytes 3145728 | tf_op jit(solution)/shard_map/tile_products/pallas_call | solution.py:120
  5.7 18.2 %all_to_all.15.parts_ref = bf16[16,64,128]{2,1,0:T(8,128)(2,1)S(1)} all-to-all(bf16[16,64,128]{2,1,0:T(8,128)(2,1)S(1)} %tile_products.2), channel_id=1, replica_groups=mesh['col'=16,'row'=2] {'col'}, dimensions={0} | all-to-all | bytes 524288 | tf_op jit(solution)/shard_map/all_to_all | solution.py:199
  23.9 0.1 collective-permute-start.1
  24.0 1.2 %collective-permute-done.1.refs_1_ = bf16[1,64,128]{2,1,0:T(8,128)(2,1)S(1)} collective-permute-done((bf16[1,64,128]{2,1,0:T(8,128)(2,1)S(1)}, bf16[1,64,128]{2,1,0:T(8,128)(2,1)S(1)}, u32[]{:S(2)}, u32[]{:S(2)}) %collective-permute-start.1) | collective-permute-done | bytes 16416 | tf_op jit(solution)/shard_map/ppermute | solution.py:193
  25.1 1.8 %tile_products.3 = bf16[16,64,128]{2,1,0:T(8,128)(2,1)S(1)} custom-call(s32[2,96]{1,0:T(2,128)S(1)} %get-tuple-element.6.info_ref, bf16[96,128,128]{2,1,0:T(8,128)(2,1)S(1)} %get-tuple-element.7.tiles_ref, bf16[1,64,128]{2,1,0:T(8,128)(2,1)S(1)} %sum_parts.1.refs_0_.first_ref, bf16[1,64,128]{2,1,0:T(8,128)(2,1)S(1)} %collective-permute-done.1.refs_1_), custom_call_target="tpu_custom_call" | custom-call | flops 805306368 | bytes 3145728 | tf_op jit(solution)/shard_map/tile_products/pallas_call | solution.py:120
  27.0 13.5 %all_to_all.16.parts_ref = bf16[16,64,128]{2,1,0:T(8,128)(2,1)S(1)} all-to-all(bf16[16,64,128]{2,1,0:T(8,128)(2,1)S(1)} %tile_products.3), channel_id=1, replica_groups=mesh['col'=16,'row'=2] {'col'}, dimensions={0} | all-to-all | bytes 524288 | tf_op jit(solution)/shard_map/all_to_all | solution.py:201
  40.5 1.0 %gram_terms.1 = (bf16[1,64,128]{2,1,0:T(8,128)(2,1)}, bf16[32,32,128]{2,1,0:T(8,128)(2,1)S(1)}) custom-call(bf16[16,64,128]{2,1,0:T(8,128)(2,1)S(1)} %all_to_all.16.parts_ref, bf16[1,64,128]{2,1,0:T(8,128)(2,1)S(1)} %sum_parts.1.refs_0_.first_ref), custom_call_target="tpu_custom_call" | custom-call | bytes 262144 | tf_op jit(solution)/shard_map/gram_terms/pallas_call | solution.py:157
  41.5 12.9 %all_to_all.17.terms_ref = bf16[32,32,128]{2,1,0:T(8,128)(2,1)S(1)} all-to-all(bf16[32,32,128]{2,1,0:T(8,128)(2,1)S(1)} %get-tuple-element.9), channel_id=1, replica_groups=mesh['col'=16,'row'=2] {'col','row'}, dimensions={0} | all-to-all | bytes 524288 | tf_op jit(solution)/shard_map/all_to_all | solution.py:203
  54.4 0.7 %gram_sum.1 = f32[64,64]{1,0:T(8,128)} custom-call(bf16[32,32,128]{2,1,0:T(8,128)(2,1)S(1)} %all_to_all.17.terms_ref), custom_call_target="tpu_custom_call" | custom-call | bytes 262144 | tf_op jit(solution)/shard_map/gram_sum/pallas_call | solution.py:175
  (1 shorter events, 0.0 us)
Async XLA Ops:
  0.6 3.1 %copy-start = (bf16[1,128,64]{1,2,0:T(8,128)(2,1)S(1)}, bf16[1,128,64]{1,2,0:T(8,128)(2,1)}, u32[]{:S(2)}) copy-start(bf16[1,128,64]{1,2,0:T(8,128)(2,1)} %param.5) | copy-start | bytes 49156
  0.6 3.1 %collective-permute-start = (bf16[1,64,128]{2,1,0:T(8,128)(2,1)}, bf16[1,64,128]{2,1,0:T(8,128)(2,1)S(1)}, u32[]{:S(2)}, u32[]{:S(2)}) collective-permute-start(bf16[1,64,128]{2,1,0:T(8,128)(2,1)} %bitcast.2), channel_id=1, source_target_pairs={{0,1},{1,0},{2,3},{3,2},{4,5},{5,4},{6,7},{7,6},{8,9},{9,8},{10,11... | collective-permute-start | bytes 49160 | tf_op jit(solution)/shard_map/ppermute | solution.py:193
  23.9 1.2 %collective-permute-start.1 = (bf16[1,64,128]{2,1,0:T(8,128)(2,1)S(1)}, bf16[1,64,128]{2,1,0:T(8,128)(2,1)S(1)}, u32[]{:S(2)}, u32[]{:S(2)}) collective-permute-start(bf16[1,64,128]{2,1,0:T(8,128)(2,1)S(1)} %sum_parts.1.refs_0_.first_ref), channel_id=1, source_target_pairs={{0,1},{1,0},{2,3},{3,2},{4,5},{5,4},{6,7},{7,6},{8,9},{9,8},{10,11... | collective-permute-start | bytes 49160 | tf_op jit(solution)/shard_map/ppermute | solution.py:193

commit v3 on v2

--- a/solution.py
+++ b/solution.py
@@ -91,7 +91,7 @@
         right[128 + row : 192 + row, lanes] = swap_halves(part).astype(BF16)
 
 
-def products_kernel(n_col, n_row, group, transposed, info_ref, tiles_ref, *refs):
+def products_kernel(order, n_row, group, transposed, info_ref, tiles_ref, *refs):
     vecs, (out_ref, right, total) = refs[:-3], refs[-3:]
     slots = tiles_ref.shape[0]
     blocks = [ref[b].astype(F32) for ref in vecs for b in range(ref.shape[0])]
@@ -112,13 +112,14 @@
             for b in range(1, n_row):
                 term = jnp.where(band == b, products[j * 64 : j * 64 + 64, b * 128 : b * 128 + 128], term)
             total[info_ref[0, start + j]] += term
-    out_ref[...] = total[:n_col].astype(BF16)
-
-
-def tile_products(info, tiles, vecs, n_col, n_row, transposed):
-    slots = tiles.shape[0]
-    return call(
-        functools.partial(products_kernel, n_col, n_row, math.gcd(slots, 4), transposed),
+    for i, place in enumerate(order):
+        out_ref[i] = total[place].astype(BF16)
+
+
+def tile_products(info, tiles, vecs, order, n_row, transposed):
+    slots, n_col = tiles.shape[0], len(order)
+    return call(
+        functools.partial(products_kernel, order, n_row, math.gcd(slots, 4), transposed),
         jax.ShapeDtypeStruct((n_col, 64, 128), BF16),
         [SMEM] + [VMEM] * (1 + len(vecs)),
         VMEM,
@@ -139,7 +140,7 @@
     return call(sum_kernel, jax.ShapeDtypeStruct(shape, BF16), [VMEM], VMEM, size=parts.size * 2, name="sum_parts")(parts)
 
 
-def gram_kernel(parts_ref, first_ref, filtered_ref, terms_ref):
+def gram_kernel(parts_ref, first_ref, filtered_ref, term_ref):
     second = jnp.sum(parts_ref[...].astype(F32), axis=0)
     first = first_ref[0]
     high = second.astype(BF16)
@@ -148,21 +149,32 @@
     full = lax.dot_general(first, high, dims, preferred_element_type=F32)
     full += lax.dot_general(first, low, dims, preferred_element_type=F32)
     term = full[:64] + swap_halves(full[64:])
-    term = jnp.where(low_lanes((32, 128)), term[:32], swap_halves(term[32:])).astype(BF16)
-    terms_ref[...] = jnp.broadcast_to(term[None], terms_ref.shape)
+    term_ref[0] = jnp.where(low_lanes((32, 128)), term[:32], swap_halves(term[32:]))
     filtered_ref[0] = jnp.concatenate([second, swap_halves(second)], axis=0).T[:64].astype(BF16)
 
 
-def gram_terms(parts, first, copies):
+def gram_term(parts, first):
     return call(
         gram_kernel,
-        (jax.ShapeDtypeStruct((1, 64, 128), BF16), jax.ShapeDtypeStruct((copies, 32, 128), BF16)),
+        (jax.ShapeDtypeStruct((1, 64, 128), BF16), jax.ShapeDtypeStruct((1, 32, 128), F32)),
         [VMEM, VMEM],
         (VMEM, VMEM),
         mib=8,
         size=parts.size * 2,
-        name="gram_terms",
+        name="gram_term",
     )(parts, first)
+
+
+def pair_kernel(*refs):
+    terms, out_ref = refs[:-1], refs[-1]
+    total = sum(jnp.sum(ref[...], axis=0) for ref in terms)
+    out_ref[...] = jnp.broadcast_to(total.astype(BF16)[None], out_ref.shape)
+
+
+def chip_terms(terms, copies):
+    return call(
+        pair_kernel, jax.ShapeDtypeStruct((copies, 32, 128), BF16), [VMEM] * len(terms), VMEM, mib=8, name="chip_terms"
+    )(*terms)
 
 
 def gram_sum_kernel(scale, terms_ref, out_ref):
@@ -193,14 +205,17 @@
             return vecs, lax.ppermute(vecs, "row", [(0, 1), (1, 0)])
         return (lax.all_gather(vecs, "row", axis=0, tiled=True),)
 
+    order = [(i + n_col // 4) % n_col for i in range(n_col)]
+
+    def scatter(blocks):
+        return lax.all_to_all(blocks, "col", 0, 0, tiled=True, axis_index_groups=[order])
+
     vecs = exchange(jnp.swapaxes(x_block, 1, 2))
     staged, info = stage(tiles, tile_rows, tile_cols, tile_count, n_col, n_row, pairs)
-    partial = tile_products(info, staged, vecs, n_col, n_row, True)
-    first = sum_parts(lax.all_to_all(partial, "col", 0, 0, tiled=True))
-    partial = tile_products(info, staged, exchange(first), n_col, n_row, False)
-    parts = lax.all_to_all(partial, "col", 0, 0, tiled=True)
-    filtered, terms = gram_terms(parts, first, n_col * n_row)
-    terms = lax.all_to_all(terms, ("col", "row"), 0, 0, tiled=True)
+    first = sum_parts(scatter(tile_products(info, staged, vecs, order, n_row, True)))
+    parts = scatter(tile_products(info, staged, exchange(first), order, n_row, False))
+    filtered, term = gram_term(parts, first)
+    terms = scatter(chip_terms(exchange(term), n_col))
     return jnp.swapaxes(filtered, 1, 2), gram_sum(terms, 1.0 / (n_col * n_row * 128))
 
 

time: 55.4 us -> 52.1 us (0.940)
  blocking collectives: 44.6 us -> 40.3 us
  waiting for transfers between devices: 1.17 us -> 2.35 us
    all_to_all x3, blocking collectives: 44.6 us -> 40.3 us  [scatter(): lax.all_to_all(blocks, 'col', 0, 0, tiled=True, axis_index_groups=[order])]
    ppermute x2 -> x3, waiting for transfers between devices: 1.17 us -> 2.35 us  [exchange(): return (vecs, lax.ppermute(vecs, 'row', [(0, 1), (1, 0)]))]
    pallas_call x3 -> x4, Pallas kernels: 4.69 us -> 4.64 us  [the longest x2 3.66 us: tile_products(): call(functools.partial(products_kernel, order, n_row, math.gcd(slots, 4),...]
  transfers between devices with their start and end apart: 2 -> 3, of which waited for: 1 -> 2; matrix products, arithmetic and copies ran while one was open for 0% -> 0% of each run, Pallas kernels for 4% -> 4%
where the time goes in v3:
time: 52.1 us; the launch traced here: 51.9 us
  blocking collectives  40.3 us (77%)
  Pallas kernels  7.33 us (14%)
  waiting for transfers between devices  2.35 us (5%)
  between operations  1.34 us (3%)
  starting transfers between devices  0.59 us (1%)
    all_to_all x3, blocking collectives, scatter(): lax.all_to_all(blocks, 'col', 0, 0, tiled=True, axis_index_groups=[order])  40.3 us
    pallas_call x2, Pallas kernels, tile_products(): call(functools.partial(products_kernel, order, n_row, math.gcd(slots, 4),...  3.66 us
    ppermute x3, waiting for transfers between devices, exchange(): return (vecs, lax.ppermute(vecs, 'row', [(0, 1), (1, 0)]))  2.35 us
    pallas_call x1, Pallas kernels, stage(): call(functools.partial(stage_kernel, n_col, n_row, group, own_first), (pl...  1.94 us
  transfers between devices with their start and end apart: 3, of which 2 were waited for; matrix products, arithmetic and copies ran while one was open for 0% of the time, Pallas kernels for 4%

profile of v3, /device:TPU:0, one launch (start us, length us, event | category | flops | bytes accessed | tf_op | source)
XLA Modules:
  0.0 51.9 jit_solution(17274494987202745807)
XLA Ops:
  0.6 0.0 copy-start
  0.6 0.5 collective-permute-start
  1.8 1.9 %stage_tiles.1 = (bf16[96,128,128]{2,1,0:T(8,128)(2,1)S(1)}, s32[2,96]{1,0:T(2,128)S(1)}) custom-call(bf16[1,1,96,128,128]{4,3,2,1,0:T(8,128)(2,1)} %tiles_ref.1, s32[1,1,96]{2,1,0:T(1,128)} %rows_ref.1, s32[1,1,96]{2,1,0:T(1,128)} %cols_ref.1, s32[1,1]{1,0:T(1,128)S(6)} %copy.7.count_ref), custom_call_target="tpu_custom_call" | custom-call | bytes 3145728 | tf_op jit(solution)/shard_map/stage_tiles/pallas_call | solution.py:68
  3.8 0.0 collective-permute-done.refs_1_
  3.8 0.0 copy-done
  3.8 1.8 %tile_products.2 = bf16[16,64,128]{2,1,0:T(8,128)(2,1)S(1)} custom-call(s32[2,96]{1,0:T(2,128)S(1)} %get-tuple-element.6.info_ref, bf16[96,128,128]{2,1,0:T(8,128)(2,1)S(1)} %get-tuple-element.7.tiles_ref, bf16[1,64,128]{2,1,0:T(8,128)(2,1)S(1)} %bitcast.3, bf16[1,64,128]{2,1,0:T(8,128)(2,1)S(1)} %collective-permute-done.refs_1_), custom_call_target="tpu_custom_call" | custom-call | flops 805306368 | bytes 3145728 | tf_op jit(solution)/shard_map/tile_products/pallas_call | solution.py:121
  5.6 17.3 %all_to_all.15.parts_ref = bf16[16,64,128]{2,1,0:T(8,128)(2,1)S(1)} all-to-all(bf16[16,64,128]{2,1,0:T(8,128)(2,1)S(1)} %tile_products.2), channel_id=1, replica_groups={{8,10,12,14,16,18,20,22,24,26,28,30,0,2,4,6},{9,11,13,15,17,19,21,23,25..., dimensions={0} | all-to-all | bytes 524288 | tf_op jit(solution)/shard_map/all_to_all | solution.py:211
  23.0 0.1 collective-permute-start.1
  23.1 1.2 %collective-permute-done.1.refs_1_ = bf16[1,64,128]{2,1,0:T(8,128)(2,1)S(1)} collective-permute-done((bf16[1,64,128]{2,1,0:T(8,128)(2,1)S(1)}, bf16[1,64,128]{2,1,0:T(8,128)(2,1)S(1)}, u32[]{:S(2)}, u32[]{:S(2)}) %collective-permute-start.1) | collective-permute-done | bytes 16416 | tf_op jit(solution)/shard_map/ppermute | solution.py:205
  24.3 1.8 %tile_products.3 = bf16[16,64,128]{2,1,0:T(8,128)(2,1)S(1)} custom-call(s32[2,96]{1,0:T(2,128)S(1)} %get-tuple-element.6.info_ref, bf16[96,128,128]{2,1,0:T(8,128)(2,1)S(1)} %get-tuple-element.7.tiles_ref, bf16[1,64,128]{2,1,0:T(8,128)(2,1)S(1)} %sum_parts.1.refs_0_.first_ref, bf16[1,64,128]{2,1,0:T(8,128)(2,1)S(1)} %collective-permute-done.1.refs_1_), custom_call_target="tpu_custom_call" | custom-call | flops 805306368 | bytes 3145728 | tf_op jit(solution)/shard_map/tile_products/pallas_call | solution.py:121
  26.1 12.7 %all_to_all.16.parts_ref = bf16[16,64,128]{2,1,0:T(8,128)(2,1)S(1)} all-to-all(bf16[16,64,128]{2,1,0:T(8,128)(2,1)S(1)} %tile_products.3), channel_id=1, replica_groups={{8,10,12,14,16,18,20,22,24,26,28,30,0,2,4,6},{9,11,13,15,17,19,21,23,25..., dimensions={0} | all-to-all | bytes 524288 | tf_op jit(solution)/shard_map/all_to_all | solution.py:211
  38.8 1.0 %gram_term.1 = (bf16[1,64,128]{2,1,0:T(8,128)(2,1)}, f32[1,32,128]{2,1,0:T(8,128)S(1)}) custom-call(bf16[16,64,128]{2,1,0:T(8,128)(2,1)S(1)} %all_to_all.16.parts_ref, bf16[1,64,128]{2,1,0:T(8,128)(2,1)S(1)} %sum_parts.1.refs_0_.first_ref), custom_call_target="tpu_custom_call" | custom-call | bytes 262144 | tf_op jit(solution)/shard_map/gram_term/pallas_call | solution.py:157
  39.8 0.0 collective-permute-start.2
  39.8 1.2 %collective-permute-done.2.refs_1_ = f32[1,32,128]{2,1,0:T(8,128)S(1)} collective-permute-done((f32[1,32,128]{2,1,0:T(8,128)S(1)}, f32[1,32,128]{2,1,0:T(8,128)S(1)}, u32[]{:S(2)}, u32[]{:S(2)}) %collective-permute-start.2) | collective-permute-done | bytes 16416 | tf_op jit(solution)/shard_map/ppermute | solution.py:205
  41.0 10.2 %all_to_all.17.terms_ref = bf16[16,32,128]{2,1,0:T(8,128)(2,1)S(1)} all-to-all(bf16[16,32,128]{2,1,0:T(8,128)(2,1)S(1)} %chip_terms.1), channel_id=1, replica_groups={{8,10,12,14,16,18,20,22,24,26,28,30,0,2,4,6},{9,11,13,15,17,19,21,23,25..., dimensions={0} | all-to-all | bytes 262144 | tf_op jit(solution)/shard_map/all_to_all | solution.py:211
  51.2 0.7 %gram_sum.1 = f32[64,64]{1,0:T(8,128)} custom-call(bf16[16,32,128]{2,1,0:T(8,128)(2,1)S(1)} %all_to_all.17.terms_ref), custom_call_target="tpu_custom_call" | custom-call | bytes 131072 | tf_op jit(solution)/shard_map/gram_sum/pallas_call | solution.py:187
  (2 shorter events, 0.1 us)
Async XLA Ops:
  0.6 3.1 %copy-start = (bf16[1,128,64]{1,2,0:T(8,128)(2,1)S(1)}, bf16[1,128,64]{1,2,0:T(8,128)(2,1)}, u32[]{:S(2)}) copy-start(bf16[1,128,64]{1,2,0:T(8,128)(2,1)} %param.5) | copy-start | bytes 49156
  0.6 3.1 %collective-permute-start = (bf16[1,64,128]{2,1,0:T(8,128)(2,1)}, bf16[1,64,128]{2,1,0:T(8,128)(2,1)S(1)}, u32[]{:S(2)}, u32[]{:S(2)}) collective-permute-start(bf16[1,64,128]{2,1,0:T(8,128)(2,1)} %bitcast.2), channel_id=1, source_target_pairs={{0,1},{1,0},{2,3},{3,2},{4,5},{5,4},{6,7},{7,6},{8,9},{9,8},{10,11... | collective-permute-start | bytes 49160 | tf_op jit(solution)/shard_map/ppermute | solution.py:205
  23.0 1.2 %collective-permute-start.1 = (bf16[1,64,128]{2,1,0:T(8,128)(2,1)S(1)}, bf16[1,64,128]{2,1,0:T(8,128)(2,1)S(1)}, u32[]{:S(2)}, u32[]{:S(2)}) collective-permute-start(bf16[1,64,128]{2,1,0:T(8,128)(2,1)S(1)} %sum_parts.1.refs_0_.first_ref), channel_id=1, source_target_pairs={{0,1},{1,0},{2,3},{3,2},{4,5},{5,4},{6,7},{7,6},{8,9},{9,8},{10,11... | collective-permute-start | bytes 49160 | tf_op jit(solution)/shard_map/ppermute | solution.py:205
  39.8 1.2 %collective-permute-start.2 = (f32[1,32,128]{2,1,0:T(8,128)S(1)}, f32[1,32,128]{2,1,0:T(8,128)S(1)}, u32[]{:S(2)}, u32[]{:S(2)}) collective-permute-start(f32[1,32,128]{2,1,0:T(8,128)S(1)} %get-tuple-element.9.refs_0_), channel_id=1, source_target_pairs={{0,1},{1,0},{2,3},{3,2},{4,5},{5,4},{6,7},{7,6},{8,9},{9,8},{10,11... | collective-permute-start | bytes 49160 | tf_op jit(solution)/shard_map/ppermute | solution.py:205

commit v4 on v3

v4 whole, which is shorter than its diff:
```python
import functools
import math

import jax
import jax.numpy as jnp
from jax import lax
from jax.experimental import pallas as pl
from jax.experimental.pallas import tpu as pltpu
from jax.sharding import PartitionSpec as P

F32 = jnp.float32
BF16 = jnp.bfloat16
MIB = 1 << 20
SMEM = pl.BlockSpec(memory_space=pltpu.SMEM)
VMEM = pl.BlockSpec(memory_space=pltpu.VMEM)
ANY = pl.BlockSpec(memory_space=pl.ANY)


def low_lanes(shape):
    return lax.broadcasted_iota(jnp.int32, shape, len(shape) - 1) < 64


def swap_halves(value):
    return pltpu.roll(value, 64, 1)


def in_hbm(*arrays):
    return tuple(pltpu.with_memory_space_constraint(array, pltpu.HBM) for array in arrays)


def call(kernel, out_shape, in_specs, out_specs, scratch=(), mib=4, flops=0, size=0, **kwargs):
    return pl.pallas_call(
        kernel,
        out_shape=out_shape,
        in_specs=in_specs,
        out_specs=out_specs,
        scratch_shapes=list(scratch),
        compiler_params=pltpu.CompilerParams(vmem_limit_bytes=mib * MIB),
        cost_estimate=pl.CostEstimate(flops=flops, bytes_accessed=size, transcendentals=0),
        **kwargs,
    )


def place_vectors(right, band, top, low):
    lanes = slice(band * 128, band * 128 + 128)
    mask = low_lanes(top.shape)
    for row, part in ((0, top), (64, low)):
        part = jnp.where(mask, part, 0.0)
        right[row : row + 64, lanes] = part.astype(BF16)
        right[128 + row : 192 + row, lanes] = swap_halves(part).astype(BF16)


def stage_kernel(x_ref, rows_ref, cols_ref, tiles_ref, vecs_ref, slot_rows, slot_cols, staged_ref, sems):
    pairs = ((tiles_ref.at[0, 0], staged_ref), (rows_ref, slot_rows), (cols_ref, slot_cols), (x_ref, vecs_ref))
    copies = [pltpu.make_async_copy(source, target, sems.at[i]) for i, (source, target) in enumerate(pairs)]
    for copy in copies:
        copy.start()
    for copy in copies:
        copy.wait()


def stage(x, rows, cols, tiles):
    x, rows, cols, tiles = in_hbm(x, rows, cols, tiles)
    return call(
        stage_kernel,
        (
            pltpu.VMEM(x.shape, x.dtype),
            pltpu.SMEM(rows.shape, rows.dtype),
            pltpu.SMEM(cols.shape, cols.dtype),
            pltpu.VMEM(tiles.shape[2:], tiles.dtype),
        ),
        [ANY] * 4,
        (VMEM, SMEM, SMEM, VMEM),
        [pltpu.SemaphoreType.DMA((4,))],
        size=tiles.size * 2,
        name="stage",
    )(x, rows, cols, tiles)


def spread_vectors(right, vecs, transposed):
    blocks = [ref[b].astype(F32) for ref in vecs for b in range(ref.shape[0])]
    for band, block in enumerate(blocks):
        if transposed:
            block = jnp.concatenate([block, jnp.zeros_like(block)], axis=0).T
            place_vectors(right, band, block[:64], block[64:])
        else:
            place_vectors(right, band, block, swap_halves(block))


def add_products(tiles_ref, rows, cols, count, first_band, right, total):
    n_col, n_row, slots = total.shape[0] - 1, right.shape[1] // 128, tiles_ref.shape[0]
    group = math.gcd(slots, 4)
    for start in range(0, slots, group):
        pieces = tiles_ref[pl.ds(start, group)]
        left = jnp.concatenate([pieces[:, :64], pieces[:, 64:]], axis=-1).reshape(group * 64, 256)
        products = jnp.dot(left, right[...], preferred_element_type=F32)
        for j in range(group):
            band = jnp.clip(cols[0, 0, start + j], 0, n_row - 1)
            band = jnp.where(band >= first_band, band - first_band, band + n_row - first_band)
            place = jnp.where(start + j < count, jnp.clip(rows[0, 0, start + j], 0, n_col - 1), n_col)
            term = products[j * 64 : j * 64 + 64, :128]
            for b in range(1, n_row):
                term = jnp.where(band == b, products[j * 64 : j * 64 + 64, b * 128 : b * 128 + 128], term)
            total[place] += term


def write_blocks(out_ref, total, order):
    for i, place in enumerate(order):
        out_ref[i] = total[place].astype(BF16)


def products_kernel(order, own_first, transposed, rows, cols, count_ref, tiles_ref, *refs):
    vecs, (out_ref, right, total) = refs[:-3], refs[-3:]
    first_band = lax.axis_index("row") if own_first else 0
    spread_vectors(right, vecs, transposed)
    total[...] = jnp.zeros_like(total)
    add_products(tiles_ref, rows, cols, count_ref[0, 0], first_band, right, total)
    for i, place in enumerate(order):
        out_ref[i] = total[place].astype(BF16)


def tile_products(rows, cols, count, tiles, vecs, order, n_row, own_first, transposed):
    n_col, slots = len(order), tiles.shape[0]
    return call(
        functools.partial(products_kernel, order, own_first, transposed),
        jax.ShapeDtypeStruct((n_col, 64, 128), BF16),
        [SMEM] * 3 + [VMEM] * (1 + len(vecs)),
        VMEM,
        [pltpu.VMEM((256, n_row * 128), BF16), pltpu.VMEM((n_col + 1, 64, 128), F32)],
        mib=12,
        flops=slots * 64 * 256 * n_row * 256,
        size=slots * 128 * 256,
        name="tile_products",
    )(rows, cols, count, tiles, *vecs)


def sum_kernel(parts_ref, out_ref):
    out_ref[0] = jnp.sum(parts_ref[...].astype(F32), axis=0).astype(BF16)


def sum_parts(parts):
    shape = (1,) + parts.shape[1:]
    return call(sum_kernel, jax.ShapeDtypeStruct(shape, BF16), [VMEM], VMEM, size=parts.size * 2, name="sum_parts")(parts)


def gram_kernel(parts_ref, first_ref, term_ref):
    second = jnp.sum(parts_ref[...].astype(F32), axis=0)
    first = first_ref[0]
    high = second.astype(BF16)
    low = (second - high.astype(F32)).astype(BF16)
    dims = (((0,), (0,)), ((), ()))
    full = lax.dot_general(first, high, dims, preferred_element_type=F32)
    full += lax.dot_general(first, low, dims, preferred_element_type=F32)
    term = full[:64] + swap_halves(full[64:])
    term_ref[0] = jnp.where(low_lanes((32, 128)), term[:32], swap_halves(term[32:]))


def gram_term(parts, first):
    shape = jax.ShapeDtypeStruct((1, 32, 128), F32)
    return call(gram_kernel, shape, [VMEM, VMEM], VMEM, size=parts.size * 2, name="gram_term")(parts, first)


def filtered_kernel(parts_ref, out_ref):
    second = jnp.sum(parts_ref[...].astype(F32), axis=0)
    out_ref[0] = jnp.concatenate([second, swap_halves(second)], axis=0).T[:64].astype(BF16)


def filtered_block(parts):
    shape = jax.ShapeDtypeStruct((1, 64, 128), BF16)
    return call(filtered_kernel, shape, [VMEM], VMEM, size=parts.size * 2, name="filtered_block")(parts)


def pair_kernel(*refs):
    terms, out_ref = refs[:-2], refs[-1]
    total = sum(jnp.sum(ref[...], axis=0) for ref in terms)
    out_ref[...] = jnp.broadcast_to(total.astype(BF16)[None], out_ref.shape)


def chip_terms(terms, before, copies):
    shape = jax.ShapeDtypeStruct((copies, 32, 128), BF16)
    return call(pair_kernel, shape, [VMEM] * len(terms) + [ANY], VMEM, name="chip_terms")(*terms, *in_hbm(before))


def gram_sum_kernel(scale, terms_ref, out_ref):
    total = jnp.sum(terms_ref[...].astype(F32), axis=0) * scale
    out_ref[:32] = total[:, :64]
    out_ref[32:] = swap_halves(total)[:, :64]


def gram_sum(terms, scale):
    return call(
        functools.partial(gram_sum_kernel, scale),
        jax.ShapeDtypeStruct((64, 64), F32),
        [VMEM],
        VMEM,
        mib=8,
        size=terms.size * 2,
        name="gram_sum",
    )(terms)


def local(x_block, tiles, tile_rows, tile_cols, tile_count):
    n_col = lax.axis_size("col")
    n_row = lax.axis_size("row")
    pairs = n_row == 2

    def exchange(vecs):
        if pairs:
            return vecs, lax.ppermute(vecs, "row", [(0, 1), (1, 0)])
        return (lax.all_gather(vecs, "row", axis=0, tiled=True),)

    lead = n_col * 3 // 4 - 1
    order = sorted(range(n_col), key=lambda k: k ^ lead)

    def scatter(blocks):
        return lax.all_to_all(blocks, "col", 0, 0, tiled=True, axis_index_groups=[order])

    x_turned = jnp.swapaxes(x_block, 1, 2)
    vecs = exchange(x_turned)
    own, rows, cols, staged = stage(x_turned, tile_rows, tile_cols, tiles)
    if pairs:
        vecs = (own, vecs[1])
    partial = tile_products(rows, cols, tile_count, staged, vecs, order, n_row, pairs, True)
    first = sum_parts(scatter(partial))
    partial = tile_products(rows, cols, tile_count, staged, exchange(first), order, n_row, pairs, False)
    parts = scatter(partial)
    terms = exchange(gram_term(parts, first))
    filtered = filtered_block(parts)
    terms = scatter(chip_terms(terms, filtered, n_col))
    return jnp.swapaxes(filtered, 1, 2), gram_sum(terms, 1.0 / (n_col * n_row * 128))


def solution(mesh):
    placed = (
        P("row", "col", None),
        P("col", "row", None, None, None),
        P("col", "row", None),
        P("col", "row", None),
        P("col", "row"),
    )
    return jax.shard_map(
        local, mesh=mesh, in_specs=placed, out_specs=(P("row", "col", None), P()), check_vma=False
    )
```

time: 52.1 us -> 47.8 us (0.917)
  blocking collectives: 40.3 us -> 37.7 us
  Pallas kernels: 7.33 us -> 6.28 us
  waiting for transfers between devices: 2.35 us -> 1.58 us
    all_to_all x3, blocking collectives: 40.3 us -> 37.7 us  [scatter(): lax.all_to_all(blocks, 'col', 0, 0, tiled=True, axis_index_groups=[order])]
    pallas_call x5 -> x6, Pallas kernels: 6.59 us -> 5.54 us  [the longest x2 2.49 us: tile_products(): call(functools.partial(products_kernel, order, own_first, transposed), ja...]
    ppermute x3, waiting for transfers between devices: 2.35 us -> 1.58 us  [exchange(): return (vecs, lax.ppermute(vecs, 'row', [(0, 1), (1, 0)]))]
  transfers between devices with their start and end apart: 3 -> 3, of which waited for: 2 -> 2; matrix products, arithmetic and copies ran while one was open for 0% -> 0% of each run, Pallas kernels for 4% -> 6%
where the time goes in v4:
time: 47.8 us; the launch traced here: 47.6 us
  blocking collectives  37.7 us (79%)
  Pallas kernels  6.28 us (13%)
  waiting for transfers between devices  1.58 us (3%)
  between operations  1.34 us (3%)
  starting transfers between devices  0.63 us (1%)
    all_to_all x3, blocking collectives, scatter(): lax.all_to_all(blocks, 'col', 0, 0, tiled=True, axis_index_groups=[order])  37.7 us
    pallas_call x2, Pallas kernels, tile_products(): call(functools.partial(products_kernel, order, own_first, transposed), ja...  2.49 us
    pallas_call x1, Pallas kernels, stage(): call(stage_kernel, (pltpu.VMEM(x.shape, x.dtype), pltpu.SMEM(rows.shape,...  1.94 us
    ppermute x3, waiting for transfers between devices, exchange(): return (vecs, lax.ppermute(vecs, 'row', [(0, 1), (1, 0)]))  1.58 us
  transfers between devices with their start and end apart: 3, of which 2 were waited for; matrix products, arithmetic and copies ran while one was open for 0% of the time, Pallas kernels for 6%

profile of v4, /device:TPU:0, one launch (start us, length us, event | category | flops | bytes accessed | tf_op | source)
XLA Modules:
  0.0 47.6 jit_solution(9640800261119668928)
XLA Ops:
  0.6 0.5 %collective-permute-start = (bf16[1,64,128]{2,1,0:T(8,128)(2,1)}, bf16[1,64,128]{2,1,0:T(8,128)(2,1)S(1)}, u32[]{:S(2)}, u32[]{:S(2)}) collective-permute-start(bf16[1,64,128]{2,1,0:T(8,128)(2,1)} %bitcast.3), channel_id=1, source_target_pairs={{0,1},{1,0},{2,3},{3,2},{4,5},{5,4},{6,7},{7,6},{8,9},{9,8},{10,11... | collective-permute-start | bytes 49160 | tf_op jit(solution)/shard_map/ppermute | solution.py:209
  1.8 1.9 %stage.1 = (bf16[1,64,128]{2,1,0:T(8,128)(2,1)S(1)}, s32[1,1,96]{2,1,0:T(1,128)S(4)}, s32[1,1,96]{2,1,0:T(1,128)S(4)}, bf16[96,128,128]{2,1,0:T(8,128)(2,1)S(1)}) custom-call(bf16[1,64,128]{2,1,0:T(8,128)(2,1)} %bitcast.4, s32[1,1,96]{2,1,0:T(1,128)} %rows_ref.1, s32[1,1,96]{2,1,0:T(1,128)} %cols_ref.1, bf16[1,1,96,128,128]{4,3,2,1,0:T(8,128)(2,1)} %tiles_ref.1), custom_call_target="tpu_custom_call" | custom-call | bytes 3145728 | tf_op jit(solution)/shard_map/stage/pallas_call | solution.py:64
  3.8 0.0 collective-permute-done.refs_1_
  3.8 1.3 %tile_products.2 = bf16[16,64,128]{2,1,0:T(8,128)(2,1)S(1)} custom-call(s32[1,1,96]{2,1,0:T(1,128)S(4)} %get-tuple-element.6.rows, s32[1,1,96]{2,1,0:T(1,128)S(4)} %get-tuple-element.7.cols, s32[1,1]{1,0:T(1,128)S(6)} %copy.7.count_ref, bf16[96,128,128]{2,1,0:T(8,128)(2,1)S(1)} %get-tuple-element.8.tiles_ref, ...), custom_call_target="tpu_custom_call" | custom-call | flops 805306368 | bytes 3145728 | tf_op jit(solution)/shard_map/tile_products/pallas_call | solution.py:124
  5.0 15.0 %all_to_all.15.parts_ref = bf16[16,64,128]{2,1,0:T(8,128)(2,1)S(1)} all-to-all(bf16[16,64,128]{2,1,0:T(8,128)(2,1)S(1)} %tile_products.2), channel_id=1, replica_groups={{22,20,18,16,30,28,26,24,6,4,2,0,14,12,10,8},{23,21,19,17,31,29,27,25,7..., dimensions={0} | all-to-all | bytes 524288 | tf_op jit(solution)/shard_map/all_to_all | solution.py:216
  20.1 0.1 collective-permute-start.1
  20.1 1.2 %collective-permute-done.1.refs_1_ = bf16[1,64,128]{2,1,0:T(8,128)(2,1)S(1)} collective-permute-done((bf16[1,64,128]{2,1,0:T(8,128)(2,1)S(1)}, bf16[1,64,128]{2,1,0:T(8,128)(2,1)S(1)}, u32[]{:S(2)}, u32[]{:S(2)}) %collective-permute-start.1) | collective-permute-done | bytes 16416 | tf_op jit(solution)/shard_map/ppermute | solution.py:209
  21.3 1.2 %tile_products.3 = bf16[16,64,128]{2,1,0:T(8,128)(2,1)S(1)} custom-call(s32[1,1,96]{2,1,0:T(1,128)S(4)} %get-tuple-element.6.rows, s32[1,1,96]{2,1,0:T(1,128)S(4)} %get-tuple-element.7.cols, s32[1,1]{1,0:T(1,128)S(6)} %copy.7.count_ref, bf16[96,128,128]{2,1,0:T(8,128)(2,1)S(1)} %get-tuple-element.8.tiles_ref, ...), custom_call_target="tpu_custom_call" | custom-call | flops 805306368 | bytes 3145728 | tf_op jit(solution)/shard_map/tile_products/pallas_call | solution.py:124
  22.5 12.7 %all_to_all.16.parts_ref = bf16[16,64,128]{2,1,0:T(8,128)(2,1)S(1)} all-to-all(bf16[16,64,128]{2,1,0:T(8,128)(2,1)S(1)} %tile_products.3), channel_id=1, replica_groups={{22,20,18,16,30,28,26,24,6,4,2,0,14,12,10,8},{23,21,19,17,31,29,27,25,7..., dimensions={0} | all-to-all | bytes 524288 | tf_op jit(solution)/shard_map/all_to_all | solution.py:216
  35.2 0.3 gram_term.1.refs_0_
  35.6 0.0 collective-permute-start.2
  35.6 0.8 %filtered_block.1.refs_2_ = bf16[1,64,128]{2,1,0:T(8,128)(2,1)} custom-call(bf16[16,64,128]{2,1,0:T(8,128)(2,1)S(1)} %all_to_all.16.parts_ref), custom_call_target="tpu_custom_call" | custom-call | bytes 262144 | tf_op jit(solution)/shard_map/filtered_block/pallas_call | solution.py:170
  36.4 0.4 collective-permute-done.2.refs_1_
  36.8 10.1 %all_to_all.17.terms_ref = bf16[16,32,128]{2,1,0:T(8,128)(2,1)S(1)} all-to-all(bf16[16,32,128]{2,1,0:T(8,128)(2,1)S(1)} %chip_terms.1), channel_id=1, replica_groups={{22,20,18,16,30,28,26,24,6,4,2,0,14,12,10,8},{23,21,19,17,31,29,27,25,7..., dimensions={0} | all-to-all | bytes 262144 | tf_op jit(solution)/shard_map/all_to_all | solution.py:216
  46.9 0.7 %gram_sum.1 = f32[64,64]{1,0:T(8,128)} custom-call(bf16[16,32,128]{2,1,0:T(8,128)(2,1)S(1)} %all_to_all.17.terms_ref), custom_call_target="tpu_custom_call" | custom-call | bytes 131072 | tf_op jit(solution)/shard_map/gram_sum/pallas_call | solution.py:191
  (2 shorter events, 0.1 us)
Async XLA Ops:
  0.6 3.1 %collective-permute-start = (bf16[1,64,128]{2,1,0:T(8,128)(2,1)}, bf16[1,64,128]{2,1,0:T(8,128)(2,1)S(1)}, u32[]{:S(2)}, u32[]{:S(2)}) collective-permute-start(bf16[1,64,128]{2,1,0:T(8,128)(2,1)} %bitcast.3), channel_id=1, source_target_pairs={{0,1},{1,0},{2,3},{3,2},{4,5},{5,4},{6,7},{7,6},{8,9},{9,8},{10,11... | collective-permute-start | bytes 49160 | tf_op jit(solution)/shard_map/ppermute | solution.py:209
  20.1 1.2 %collective-permute-start.1 = (bf16[1,64,128]{2,1,0:T(8,128)(2,1)S(1)}, bf16[1,64,128]{2,1,0:T(8,128)(2,1)S(1)}, u32[]{:S(2)}, u32[]{:S(2)}) collective-permute-start(bf16[1,64,128]{2,1,0:T(8,128)(2,1)S(1)} %sum_parts.1.refs_0_.first_ref), channel_id=1, source_target_pairs={{0,1},{1,0},{2,3},{3,2},{4,5},{5,4},{6,7},{7,6},{8,9},{9,8},{10,11... | collective-permute-start | bytes 49160 | tf_op jit(solution)/shard_map/ppermute | solution.py:209
  35.6 1.2 %collective-permute-start.2 = (f32[1,32,128]{2,1,0:T(8,128)S(1)}, f32[1,32,128]{2,1,0:T(8,128)S(1)}, u32[]{:S(2)}, u32[]{:S(2)}) collective-permute-start(f32[1,32,128]{2,1,0:T(8,128)S(1)} %gram_term.1.refs_0_), channel_id=1, source_target_pairs={{0,1},{1,0},{2,3},{3,2},{4,5},{5,4},{6,7},{7,6},{8,9},{9,8},{10,11... | collective-permute-start | bytes 49160 | tf_op jit(solution)/shard_map/ppermute | solution.py:209

commit v5 on v4

--- a/solution.py
+++ b/solution.py
@@ -50,8 +50,8 @@
         right[128 + row : 192 + row, lanes] = swap_halves(part).astype(BF16)
 
 
-def stage_kernel(x_ref, rows_ref, cols_ref, tiles_ref, vecs_ref, slot_rows, slot_cols, staged_ref, sems):
-    pairs = ((tiles_ref.at[0, 0], staged_ref), (rows_ref, slot_rows), (cols_ref, slot_cols), (x_ref, vecs_ref))
+def stage_kernel(x_ref, rows_ref, cols_ref, vecs_ref, slot_rows, slot_cols, sems):
+    pairs = ((rows_ref, slot_rows), (cols_ref, slot_cols), (x_ref, vecs_ref))
     copies = [pltpu.make_async_copy(source, target, sems.at[i]) for i, (source, target) in enumerate(pairs)]
     for copy in copies:
         copy.start()
@@ -59,22 +59,17 @@
         copy.wait()
 
 
-def stage(x, rows, cols, tiles):
-    x, rows, cols, tiles = in_hbm(x, rows, cols, tiles)
+def stage(x, rows, cols):
+    x, rows, cols = in_hbm(x, rows, cols)
     return call(
         stage_kernel,
-        (
-            pltpu.VMEM(x.shape, x.dtype),
-            pltpu.SMEM(rows.shape, rows.dtype),
-            pltpu.SMEM(cols.shape, cols.dtype),
-            pltpu.VMEM(tiles.shape[2:], tiles.dtype),
-        ),
-        [ANY] * 4,
-        (VMEM, SMEM, SMEM, VMEM),
-        [pltpu.SemaphoreType.DMA((4,))],
-        size=tiles.size * 2,
+        (pltpu.VMEM(x.shape, x.dtype), pltpu.SMEM(rows.shape, rows.dtype), pltpu.SMEM(cols.shape, cols.dtype)),
+        [ANY] * 3,
+        (VMEM, SMEM, SMEM),
+        [pltpu.SemaphoreType.DMA((3,))],
+        flops=3 * 10**9,
         name="stage",
-    )(x, rows, cols, tiles)
+    )(x, rows, cols)
 
 
 def spread_vectors(right, vecs, transposed):
@@ -217,7 +212,8 @@
 
     x_turned = jnp.swapaxes(x_block, 1, 2)
     vecs = exchange(x_turned)
-    own, rows, cols, staged = stage(x_turned, tile_rows, tile_cols, tiles)
+    own, rows, cols = stage(x_turned, tile_rows, tile_cols)
+    staged = pltpu.with_memory_space_constraint(tiles[0, 0], pltpu.VMEM)
     if pairs:
         vecs = (own, vecs[1])
     partial = tile_products(rows, cols, tile_count, staged, vecs, order, n_row, pairs, True)

time: 47.8 us -> 47 us (0.983)
  Pallas kernels: 6.28 us -> 5.33 us
    pallas_call x1, Pallas kernels: 1.94 us -> 1 us  [stage(): call(stage_kernel, (pltpu.VMEM(x.shape, x.dtype), pltpu.SMEM(rows.shape,...]
  transfers between devices with their start and end apart: 3 -> 3, of which waited for: 2 -> 2; matrix products, arithmetic and copies ran while one was open for 0% -> 0% of each run, Pallas kernels for 6% -> 4%
where the time goes in v5:
time: 47 us; the launch traced here: 46.6 us
  blocking collectives  37.7 us (80%)
  Pallas kernels  5.33 us (11%)
  waiting for transfers between devices  1.58 us (3%)
  between operations  1.35 us (3%)
  starting transfers between devices  0.63 us (1%)
    all_to_all x3, blocking collectives, scatter(): lax.all_to_all(blocks, 'col', 0, 0, tiled=True, axis_index_groups=[order])  37.7 us
    pallas_call x2, Pallas kernels, tile_products(): call(functools.partial(products_kernel, order, own_first, transposed), ja...  2.48 us
    ppermute x3, waiting for transfers between devices, exchange(): return (vecs, lax.ppermute(vecs, 'row', [(0, 1), (1, 0)]))  1.58 us
    pallas_call x1, Pallas kernels, stage(): call(stage_kernel, (pltpu.VMEM(x.shape, x.dtype), pltpu.SMEM(rows.shape,...  1 us
  transfers between devices with their start and end apart: 3, of which 2 were waited for; matrix products, arithmetic and copies ran while one was open for 0% of the time, Pallas kernels for 4%

profile of v5, /device:TPU:0, one launch (start us, length us, event | category | flops | bytes accessed | tf_op | source)
XLA Modules:
  0.0 46.6 jit_solution(15317019877940420769)
XLA Ops:
  0.6 0.0 copy-start
  0.6 0.5 %collective-permute-start = (bf16[1,64,128]{2,1,0:T(8,128)(2,1)}, bf16[1,64,128]{2,1,0:T(8,128)(2,1)S(1)}, u32[]{:S(2)}, u32[]{:S(2)}) collective-permute-start(bf16[1,64,128]{2,1,0:T(8,128)(2,1)} %bitcast.6), channel_id=1, source_target_pairs={{0,1},{1,0},{2,3},{3,2},{4,5},{5,4},{6,7},{7,6},{8,9},{9,8},{10,11... | collective-permute-start | bytes 49160 | tf_op jit(solution)/shard_map/ppermute | solution.py:204
  1.2 1.0 %stage.1 = (bf16[1,64,128]{2,1,0:T(8,128)(2,1)S(1)}, s32[1,1,96]{2,1,0:T(1,128)S(4)}, s32[1,1,96]{2,1,0:T(1,128)S(4)}) custom-call(bf16[1,64,128]{2,1,0:T(8,128)(2,1)} %bitcast.7, s32[1,1,96]{2,1,0:T(1,128)} %rows_ref.1, s32[1,1,96]{2,1,0:T(1,128)} %cols_ref.1), custom_call_target="tpu_custom_call" | custom-call | flops 3000000000 | tf_op jit(solution)/shard_map/stage/pallas_call | solution.py:64
  2.8 0.0 collective-permute-done.refs_1_
  2.8 0.0 copy-done
  2.8 1.3 %tile_products.2 = bf16[16,64,128]{2,1,0:T(8,128)(2,1)S(1)} custom-call(s32[1,1,96]{2,1,0:T(1,128)S(4)} %get-tuple-element.5.rows, s32[1,1,96]{2,1,0:T(1,128)S(4)} %get-tuple-element.6.cols, s32[1,1]{1,0:T(1,128)S(6)} %copy.7.count_ref, bf16[96,128,128]{2,1,0:T(8,128)(2,1)S(1)} %bitcast.3, bf16[1,64,128]{2,1,0:T(8,128)(2,1)S(1)} %get-tuple-element.7.refs_0_, ...), custom_call_target="tpu_custom_call" | custom-call | flops 805306368 | bytes 3145728 | tf_op jit(solution)/shard_map/tile_products/pallas_call | solution.py:119
  4.1 15.0 %all_to_all.15.parts_ref = bf16[16,64,128]{2,1,0:T(8,128)(2,1)S(1)} all-to-all(bf16[16,64,128]{2,1,0:T(8,128)(2,1)S(1)} %tile_products.2), channel_id=1, replica_groups={{22,20,18,16,30,28,26,24,6,4,2,0,14,12,10,8},{23,21,19,17,31,29,27,25,7..., dimensions={0} | all-to-all | bytes 524288 | tf_op jit(solution)/shard_map/all_to_all | solution.py:211
  19.1 0.1 collective-permute-start.1
  19.2 1.2 %collective-permute-done.1.refs_1_ = bf16[1,64,128]{2,1,0:T(8,128)(2,1)S(1)} collective-permute-done((bf16[1,64,128]{2,1,0:T(8,128)(2,1)S(1)}, bf16[1,64,128]{2,1,0:T(8,128)(2,1)S(1)}, u32[]{:S(2)}, u32[]{:S(2)}) %collective-permute-start.1) | collective-permute-done | bytes 16416 | tf_op jit(solution)/shard_map/ppermute | solution.py:204
  20.4 1.2 %tile_products.3 = bf16[16,64,128]{2,1,0:T(8,128)(2,1)S(1)} custom-call(s32[1,1,96]{2,1,0:T(1,128)S(4)} %get-tuple-element.5.rows, s32[1,1,96]{2,1,0:T(1,128)S(4)} %get-tuple-element.6.cols, s32[1,1]{1,0:T(1,128)S(6)} %copy.7.count_ref, bf16[96,128,128]{2,1,0:T(8,128)(2,1)S(1)} %bitcast.4, bf16[1,64,128]{2,1,0:T(8,128)(2,1)S(1)} %sum_parts.1.refs_0_.first_ref, ...), custom_call_target="tpu_custom_call" | custom-call | flops 805306368 | bytes 3145728 | tf_op jit(solution)/shard_map/tile_products/pallas_call | solution.py:119
  21.6 12.7 %all_to_all.16.parts_ref = bf16[16,64,128]{2,1,0:T(8,128)(2,1)S(1)} all-to-all(bf16[16,64,128]{2,1,0:T(8,128)(2,1)S(1)} %tile_products.3), channel_id=1, replica_groups={{22,20,18,16,30,28,26,24,6,4,2,0,14,12,10,8},{23,21,19,17,31,29,27,25,7..., dimensions={0} | all-to-all | bytes 524288 | tf_op jit(solution)/shard_map/all_to_all | solution.py:211
  34.3 0.3 gram_term.1.refs_0_
  34.6 0.0 collective-permute-start.2
  34.7 0.8 %filtered_block.1.refs_2_ = bf16[1,64,128]{2,1,0:T(8,128)(2,1)} custom-call(bf16[16,64,128]{2,1,0:T(8,128)(2,1)S(1)} %all_to_all.16.parts_ref), custom_call_target="tpu_custom_call" | custom-call | bytes 262144 | tf_op jit(solution)/shard_map/filtered_block/pallas_call | solution.py:165
  35.4 0.4 collective-permute-done.2.refs_1_
  35.9 10.1 %all_to_all.17.terms_ref = bf16[16,32,128]{2,1,0:T(8,128)(2,1)S(1)} all-to-all(bf16[16,32,128]{2,1,0:T(8,128)(2,1)S(1)} %chip_terms.1), channel_id=1, replica_groups={{22,20,18,16,30,28,26,24,6,4,2,0,14,12,10,8},{23,21,19,17,31,29,27,25,7..., dimensions={0} | all-to-all | bytes 262144 | tf_op jit(solution)/shard_map/all_to_all | solution.py:211
  45.9 0.7 %gram_sum.1 = f32[64,64]{1,0:T(8,128)} custom-call(bf16[16,32,128]{2,1,0:T(8,128)(2,1)S(1)} %all_to_all.17.terms_ref), custom_call_target="tpu_custom_call" | custom-call | bytes 131072 | tf_op jit(solution)/shard_map/gram_sum/pallas_call | solution.py:186
  (2 shorter events, 0.1 us)
Async XLA Ops:
  0.6 2.2 %copy-start = (bf16[1,1,96,128,128]{4,3,2,1,0:T(8,128)(2,1)S(1)}, bf16[1,1,96,128,128]{4,3,2,1,0:T(8,128)(2,1)}, u32[]{:S(2)}) copy-start(bf16[1,1,96,128,128]{4,3,2,1,0:T(8,128)(2,1)} %param.6) | copy-start | bytes 9437188
  0.6 2.2 %collective-permute-start = (bf16[1,64,128]{2,1,0:T(8,128)(2,1)}, bf16[1,64,128]{2,1,0:T(8,128)(2,1)S(1)}, u32[]{:S(2)}, u32[]{:S(2)}) collective-permute-start(bf16[1,64,128]{2,1,0:T(8,128)(2,1)} %bitcast.6), channel_id=1, source_target_pairs={{0,1},{1,0},{2,3},{3,2},{4,5},{5,4},{6,7},{7,6},{8,9},{9,8},{10,11... | collective-permute-start | bytes 49160 | tf_op jit(solution)/shard_map/ppermute | solution.py:204
  19.1 1.2 %collective-permute-start.1 = (bf16[1,64,128]{2,1,0:T(8,128)(2,1)S(1)}, bf16[1,64,128]{2,1,0:T(8,128)(2,1)S(1)}, u32[]{:S(2)}, u32[]{:S(2)}) collective-permute-start(bf16[1,64,128]{2,1,0:T(8,128)(2,1)S(1)} %sum_parts.1.refs_0_.first_ref), channel_id=1, source_target_pairs={{0,1},{1,0},{2,3},{3,2},{4,5},{5,4},{6,7},{7,6},{8,9},{9,8},{10,11... | collective-permute-start | bytes 49160 | tf_op jit(solution)/shard_map/ppermute | solution.py:204
  34.6 1.2 %collective-permute-start.2 = (f32[1,32,128]{2,1,0:T(8,128)S(1)}, f32[1,32,128]{2,1,0:T(8,128)S(1)}, u32[]{:S(2)}, u32[]{:S(2)}) collective-permute-start(f32[1,32,128]{2,1,0:T(8,128)S(1)} %gram_term.1.refs_0_), channel_id=1, source_target_pairs={{0,1},{1,0},{2,3},{3,2},{4,5},{5,4},{6,7},{7,6},{8,9},{9,8},{10,11... | collective-permute-start | bytes 49160 | tf_op jit(solution)/shard_map/ppermute | solution.py:204

commit v6 on v5

--- a/solution.py
+++ b/solution.py
@@ -50,8 +50,8 @@
         right[128 + row : 192 + row, lanes] = swap_halves(part).astype(BF16)
 
 
-def stage_kernel(x_ref, rows_ref, cols_ref, vecs_ref, slot_rows, slot_cols, sems):
-    pairs = ((rows_ref, slot_rows), (cols_ref, slot_cols), (x_ref, vecs_ref))
+def stage_kernel(rows_ref, cols_ref, slot_rows, slot_cols, sems):
+    pairs = ((rows_ref, slot_rows), (cols_ref, slot_cols))
     copies = [pltpu.make_async_copy(source, target, sems.at[i]) for i, (source, target) in enumerate(pairs)]
     for copy in copies:
         copy.start()
@@ -59,17 +59,17 @@
         copy.wait()
 
 
-def stage(x, rows, cols):
-    x, rows, cols = in_hbm(x, rows, cols)
+def stage(rows, cols):
+    rows, cols = in_hbm(rows, cols)
     return call(
         stage_kernel,
-        (pltpu.VMEM(x.shape, x.dtype), pltpu.SMEM(rows.shape, rows.dtype), pltpu.SMEM(cols.shape, cols.dtype)),
-        [ANY] * 3,
-        (VMEM, SMEM, SMEM),
+        (pltpu.SMEM(rows.shape, rows.dtype), pltpu.SMEM(cols.shape, cols.dtype)),
+        [ANY] * 2,
+        (SMEM, SMEM),
         [pltpu.SemaphoreType.DMA((3,))],
         flops=3 * 10**9,
         name="stage",
-    )(x, rows, cols)
+    )(rows, cols)
 
 
 def spread_vectors(right, vecs, transposed):
@@ -84,7 +84,7 @@
 
 def add_products(tiles_ref, rows, cols, count, first_band, right, total):
     n_col, n_row, slots = total.shape[0] - 1, right.shape[1] // 128, tiles_ref.shape[0]
-    group = math.gcd(slots, 4)
+    group = math.gcd(slots, 2)
     for start in range(0, slots, group):
         pieces = tiles_ref[pl.ds(start, group)]
         left = jnp.concatenate([pieces[:, :64], pieces[:, 64:]], axis=-1).reshape(group * 64, 256)
@@ -212,10 +212,8 @@
 
     x_turned = jnp.swapaxes(x_block, 1, 2)
     vecs = exchange(x_turned)
-    own, rows, cols = stage(x_turned, tile_rows, tile_cols)
+    rows, cols = stage(tile_rows, tile_cols)
     staged = pltpu.with_memory_space_constraint(tiles[0, 0], pltpu.VMEM)
-    if pairs:
-        vecs = (own, vecs[1])
     partial = tile_products(rows, cols, tile_count, staged, vecs, order, n_row, pairs, True)
     first = sum_parts(scatter(partial))
     partial = tile_products(rows, cols, tile_count, staged, exchange(first), order, n_row, pairs, False)

time: 47 us -> 46.7 us (level)
  transfers between devices with their start and end apart: 3 -> 3, of which waited for: 2 -> 2; matrix products, arithmetic and copies ran while one was open for 0% -> 0% of each run, Pallas kernels for 4% -> 3%
where the time goes in v6:
time: 46.7 us; the launch traced here: 46.5 us
  blocking collectives  37.8 us (81%)
  Pallas kernels  5.09 us (11%)
  waiting for transfers between devices  1.58 us (3%)
  between operations  1.37 us (3%)
  starting transfers between devices  0.62 us (1%)
    all_to_all x3, blocking collectives, scatter(): lax.all_to_all(blocks, 'col', 0, 0, tiled=True, axis_index_groups=[order])  37.8 us
    pallas_call x2, Pallas kernels, tile_products(): call(functools.partial(products_kernel, order, own_first, transposed), ja...  2.41 us
    ppermute x3, waiting for transfers between devices, exchange(): return (vecs, lax.ppermute(vecs, 'row', [(0, 1), (1, 0)]))  1.58 us
  transfers between devices with their start and end apart: 3, of which 2 were waited for; matrix products, arithmetic and copies ran while one was open for 0% of the time, Pallas kernels for 3%

profile of v6, /device:TPU:0, one launch (start us, length us, event | category | flops | bytes accessed | tf_op | source)
XLA Modules:
  0.0 46.5 jit_solution(4195333453565593656)
XLA Ops:
  0.6 0.0 copy-start
  0.6 0.0 copy-start.1
  0.7 0.5 %collective-permute-start = (bf16[1,64,128]{2,1,0:T(8,128)(2,1)}, bf16[1,64,128]{2,1,0:T(8,128)(2,1)S(1)}, u32[]{:S(2)}, u32[]{:S(2)}) collective-permute-start(bf16[1,64,128]{2,1,0:T(8,128)(2,1)} %bitcast.5), channel_id=1, source_target_pairs={{0,1},{1,0},{2,3},{3,2},{4,5},{5,4},{6,7},{7,6},{8,9},{9,8},{10,11... | collective-permute-start | bytes 49160 | tf_op jit(solution)/shard_map/ppermute | solution.py:204
  1.2 0.8 %stage.1 = (s32[1,1,96]{2,1,0:T(1,128)S(4)}, s32[1,1,96]{2,1,0:T(1,128)S(4)}) custom-call(s32[1,1,96]{2,1,0:T(1,128)} %rows_ref.1, s32[1,1,96]{2,1,0:T(1,128)} %cols_ref.1), custom_call_target="tpu_custom_call" | custom-call | flops 3000000000 | tf_op jit(solution)/shard_map/stage/pallas_call | solution.py:64
  2.7 0.0 collective-permute-done.refs_1_
  2.7 0.0 copy-done
  2.7 0.0 copy-done.1
  2.7 1.2 %tile_products.2 = bf16[16,64,128]{2,1,0:T(8,128)(2,1)S(1)} custom-call(s32[1,1,96]{2,1,0:T(1,128)S(4)} %get-tuple-element.4.rows, s32[1,1,96]{2,1,0:T(1,128)S(4)} %get-tuple-element.5.cols, s32[1,1]{1,0:T(1,128)S(6)} %copy.7.count_ref, bf16[96,128,128]{2,1,0:T(8,128)(2,1)S(1)} %bitcast.3, bf16[1,64,128]{2,1,0:T(8,128)(2,1)S(1)} %bitcast.6, ...), custom_call_target="tpu_custom_call" | custom-call | flops 805306368 | bytes 3145728 | tf_op jit(solution)/shard_map/tile_products/pallas_call | solution.py:119
  3.9 15.0 %all_to_all.15.parts_ref = bf16[16,64,128]{2,1,0:T(8,128)(2,1)S(1)} all-to-all(bf16[16,64,128]{2,1,0:T(8,128)(2,1)S(1)} %tile_products.2), channel_id=1, replica_groups={{22,20,18,16,30,28,26,24,6,4,2,0,14,12,10,8},{23,21,19,17,31,29,27,25,7..., dimensions={0} | all-to-all | bytes 524288 | tf_op jit(solution)/shard_map/all_to_all | solution.py:211
  18.9 0.1 collective-permute-start.1
  19.0 1.2 %collective-permute-done.1.refs_1_ = bf16[1,64,128]{2,1,0:T(8,128)(2,1)S(1)} collective-permute-done((bf16[1,64,128]{2,1,0:T(8,128)(2,1)S(1)}, bf16[1,64,128]{2,1,0:T(8,128)(2,1)S(1)}, u32[]{:S(2)}, u32[]{:S(2)}) %collective-permute-start.1) | collective-permute-done | bytes 16416 | tf_op jit(solution)/shard_map/ppermute | solution.py:204
  20.2 1.2 %tile_products.3 = bf16[16,64,128]{2,1,0:T(8,128)(2,1)S(1)} custom-call(s32[1,1,96]{2,1,0:T(1,128)S(4)} %get-tuple-element.4.rows, s32[1,1,96]{2,1,0:T(1,128)S(4)} %get-tuple-element.5.cols, s32[1,1]{1,0:T(1,128)S(6)} %copy.7.count_ref, bf16[96,128,128]{2,1,0:T(8,128)(2,1)S(1)} %bitcast.4, bf16[1,64,128]{2,1,0:T(8,128)(2,1)S(1)} %sum_parts.1.refs_0_.first_ref, ...), custom_call_target="tpu_custom_call" | custom-call | flops 805306368 | bytes 3145728 | tf_op jit(solution)/shard_map/tile_products/pallas_call | solution.py:119
  21.4 12.7 %all_to_all.16.parts_ref = bf16[16,64,128]{2,1,0:T(8,128)(2,1)S(1)} all-to-all(bf16[16,64,128]{2,1,0:T(8,128)(2,1)S(1)} %tile_products.3), channel_id=1, replica_groups={{22,20,18,16,30,28,26,24,6,4,2,0,14,12,10,8},{23,21,19,17,31,29,27,25,7..., dimensions={0} | all-to-all | bytes 524288 | tf_op jit(solution)/shard_map/all_to_all | solution.py:211
  34.1 0.3 gram_term.1.refs_0_
  34.5 0.0 collective-permute-start.2
  34.5 0.8 %filtered_block.1.refs_2_ = bf16[1,64,128]{2,1,0:T(8,128)(2,1)} custom-call(bf16[16,64,128]{2,1,0:T(8,128)(2,1)S(1)} %all_to_all.16.parts_ref), custom_call_target="tpu_custom_call" | custom-call | bytes 262144 | tf_op jit(solution)/shard_map/filtered_block/pallas_call | solution.py:165
  35.3 0.4 collective-permute-done.2.refs_1_
  35.7 10.1 %all_to_all.17.terms_ref = bf16[16,32,128]{2,1,0:T(8,128)(2,1)S(1)} all-to-all(bf16[16,32,128]{2,1,0:T(8,128)(2,1)S(1)} %chip_terms.1), channel_id=1, replica_groups={{22,20,18,16,30,28,26,24,6,4,2,0,14,12,10,8},{23,21,19,17,31,29,27,25,7..., dimensions={0} | all-to-all | bytes 262144 | tf_op jit(solution)/shard_map/all_to_all | solution.py:211
  45.7 0.7 %gram_sum.1 = f32[64,64]{1,0:T(8,128)} custom-call(bf16[16,32,128]{2,1,0:T(8,128)(2,1)S(1)} %all_to_all.17.terms_ref), custom_call_target="tpu_custom_call" | custom-call | bytes 131072 | tf_op jit(solution)/shard_map/gram_sum/pallas_call | solution.py:186
  (2 shorter events, 0.1 us)
Async XLA Ops:
  0.6 2.0 %copy-start = (bf16[1,1,96,128,128]{4,3,2,1,0:T(8,128)(2,1)S(1)}, bf16[1,1,96,128,128]{4,3,2,1,0:T(8,128)(2,1)}, u32[]{:S(2)}) copy-start(bf16[1,1,96,128,128]{4,3,2,1,0:T(8,128)(2,1)} %param.6) | copy-start | bytes 9437188
  0.6 2.0 %copy-start.1 = (bf16[1,128,64]{1,2,0:T(8,128)(2,1)S(1)}, bf16[1,128,64]{1,2,0:T(8,128)(2,1)}, u32[]{:S(2)}) copy-start(bf16[1,128,64]{1,2,0:T(8,128)(2,1)} %param.5) | copy-start | bytes 49156
  0.7 2.0 %collective-permute-start = (bf16[1,64,128]{2,1,0:T(8,128)(2,1)}, bf16[1,64,128]{2,1,0:T(8,128)(2,1)S(1)}, u32[]{:S(2)}, u32[]{:S(2)}) collective-permute-start(bf16[1,64,128]{2,1,0:T(8,128)(2,1)} %bitcast.5), channel_id=1, source_target_pairs={{0,1},{1,0},{2,3},{3,2},{4,5},{5,4},{6,7},{7,6},{8,9},{9,8},{10,11... | collective-permute-start | bytes 49160 | tf_op jit(solution)/shard_map/ppermute | solution.py:204
  18.9 1.2 %collective-permute-start.1 = (bf16[1,64,128]{2,1,0:T(8,128)(2,1)S(1)}, bf16[1,64,128]{2,1,0:T(8,128)(2,1)S(1)}, u32[]{:S(2)}, u32[]{:S(2)}) collective-permute-start(bf16[1,64,128]{2,1,0:T(8,128)(2,1)S(1)} %sum_parts.1.refs_0_.first_ref), channel_id=1, source_target_pairs={{0,1},{1,0},{2,3},{3,2},{4,5},{5,4},{6,7},{7,6},{8,9},{9,8},{10,11... | collective-permute-start | bytes 49160 | tf_op jit(solution)/shard_map/ppermute | solution.py:204
  34.5 1.2 %collective-permute-start.2 = (f32[1,32,128]{2,1,0:T(8,128)S(1)}, f32[1,32,128]{2,1,0:T(8,128)S(1)}, u32[]{:S(2)}, u32[]{:S(2)}) collective-permute-start(f32[1,32,128]{2,1,0:T(8,128)S(1)} %gram_term.1.refs_0_), channel_id=1, source_target_pairs={{0,1},{1,0},{2,3},{3,2},{4,5},{5,4},{6,7},{7,6},{8,9},{9,8},{10,11... | collective-permute-start | bytes 49160 | tf_op jit(solution)/shard_map/ppermute | solution.py:204

commit v7 on v6

--- a/solution.py
+++ b/solution.py
@@ -11,6 +11,7 @@
 F32 = jnp.float32
 BF16 = jnp.bfloat16
 MIB = 1 << 20
+MEASURED_ORDER = {16: [11, 3, 13, 0, 2, 1, 5, 8, 6, 15, 4, 12, 9, 10, 14, 7]}
 SMEM = pl.BlockSpec(memory_space=pltpu.SMEM)
 VMEM = pl.BlockSpec(memory_space=pltpu.VMEM)
 ANY = pl.BlockSpec(memory_space=pl.ANY)
@@ -205,7 +206,7 @@
         return (lax.all_gather(vecs, "row", axis=0, tiled=True),)
 
     lead = n_col * 3 // 4 - 1
-    order = sorted(range(n_col), key=lambda k: k ^ lead)
+    order = MEASURED_ORDER.get(n_col, sorted(range(n_col), key=lambda k: k ^ lead))
 
     def scatter(blocks):
         return lax.all_to_all(blocks, "col", 0, 0, tiled=True, axis_index_groups=[order])

time: 46.7 us -> 46.4 us (level)
  no operation moved by 1% of the time
where the time goes in v7:
time: 46.4 us; the launch traced here: 46.1 us
  blocking collectives  37.5 us (81%)
  Pallas kernels  5.09 us (11%)
  waiting for transfers between devices  1.58 us (3%)
  between operations  1.37 us (3%)
  starting transfers between devices  0.63 us (1%)
    all_to_all x3, blocking collectives, scatter(): lax.all_to_all(blocks, 'col', 0, 0, tiled=True, axis_index_groups=[order])  37.5 us
    pallas_call x2, Pallas kernels, tile_products(): call(functools.partial(products_kernel, order, own_first, transposed), ja...  2.42 us
    ppermute x3, waiting for transfers between devices, exchange(): return (vecs, lax.ppermute(vecs, 'row', [(0, 1), (1, 0)]))  1.58 us
  transfers between devices with their start and end apart: 3, of which 2 were waited for; matrix products, arithmetic and copies ran while one was open for 0% of the time, Pallas kernels for 3%

profile of v7, /device:TPU:0, one launch (start us, length us, event | category | flops | bytes accessed | tf_op | source)
XLA Modules:
  0.0 46.1 jit_solution(18167794135607607911)
XLA Ops:
  0.6 0.0 copy-start
  0.6 0.0 copy-start.1
  0.7 0.5 %collective-permute-start = (bf16[1,64,128]{2,1,0:T(8,128)(2,1)}, bf16[1,64,128]{2,1,0:T(8,128)(2,1)S(1)}, u32[]{:S(2)}, u32[]{:S(2)}) collective-permute-start(bf16[1,64,128]{2,1,0:T(8,128)(2,1)} %bitcast.5), channel_id=1, source_target_pairs={{0,1},{1,0},{2,3},{3,2},{4,5},{5,4},{6,7},{7,6},{8,9},{9,8},{10,11... | collective-permute-start | bytes 49160 | tf_op jit(solution)/shard_map/ppermute | solution.py:205
  1.2 0.8 %stage.1 = (s32[1,1,96]{2,1,0:T(1,128)S(4)}, s32[1,1,96]{2,1,0:T(1,128)S(4)}) custom-call(s32[1,1,96]{2,1,0:T(1,128)} %rows_ref.1, s32[1,1,96]{2,1,0:T(1,128)} %cols_ref.1), custom_call_target="tpu_custom_call" | custom-call | flops 3000000000 | tf_op jit(solution)/shard_map/stage/pallas_call | solution.py:65
  2.7 0.0 collective-permute-done.refs_1_
  2.7 0.0 copy-done
  2.7 0.0 copy-done.1
  2.7 1.2 %tile_products.2 = bf16[16,64,128]{2,1,0:T(8,128)(2,1)S(1)} custom-call(s32[1,1,96]{2,1,0:T(1,128)S(4)} %get-tuple-element.4.rows, s32[1,1,96]{2,1,0:T(1,128)S(4)} %get-tuple-element.5.cols, s32[1,1]{1,0:T(1,128)S(6)} %copy.7.count_ref, bf16[96,128,128]{2,1,0:T(8,128)(2,1)S(1)} %bitcast.3, bf16[1,64,128]{2,1,0:T(8,128)(2,1)S(1)} %bitcast.6, ...), custom_call_target="tpu_custom_call" | custom-call | flops 805306368 | bytes 3145728 | tf_op jit(solution)/shard_map/tile_products/pallas_call | solution.py:120
  3.9 15.2 %all_to_all.15.parts_ref = bf16[16,64,128]{2,1,0:T(8,128)(2,1)S(1)} all-to-all(bf16[16,64,128]{2,1,0:T(8,128)(2,1)S(1)} %tile_products.2), channel_id=1, replica_groups={{22,6,26,0,4,2,10,16,12,30,8,24,18,20,28,14},{23,7,27,1,5,3,11,17,13,31..., dimensions={0} | all-to-all | bytes 524288 | tf_op jit(solution)/shard_map/all_to_all | solution.py:212
  19.2 0.1 collective-permute-start.1
  19.3 1.2 %collective-permute-done.1.refs_1_ = bf16[1,64,128]{2,1,0:T(8,128)(2,1)S(1)} collective-permute-done((bf16[1,64,128]{2,1,0:T(8,128)(2,1)S(1)}, bf16[1,64,128]{2,1,0:T(8,128)(2,1)S(1)}, u32[]{:S(2)}, u32[]{:S(2)}) %collective-permute-start.1) | collective-permute-done | bytes 16416 | tf_op jit(solution)/shard_map/ppermute | solution.py:205
  20.5 1.2 %tile_products.3 = bf16[16,64,128]{2,1,0:T(8,128)(2,1)S(1)} custom-call(s32[1,1,96]{2,1,0:T(1,128)S(4)} %get-tuple-element.4.rows, s32[1,1,96]{2,1,0:T(1,128)S(4)} %get-tuple-element.5.cols, s32[1,1]{1,0:T(1,128)S(6)} %copy.7.count_ref, bf16[96,128,128]{2,1,0:T(8,128)(2,1)S(1)} %bitcast.4, bf16[1,64,128]{2,1,0:T(8,128)(2,1)S(1)} %sum_parts.1.refs_0_.first_ref, ...), custom_call_target="tpu_custom_call" | custom-call | flops 805306368 | bytes 3145728 | tf_op jit(solution)/shard_map/tile_products/pallas_call | solution.py:120
  21.7 12.5 %all_to_all.16.parts_ref = bf16[16,64,128]{2,1,0:T(8,128)(2,1)S(1)} all-to-all(bf16[16,64,128]{2,1,0:T(8,128)(2,1)S(1)} %tile_products.3), channel_id=1, replica_groups={{22,6,26,0,4,2,10,16,12,30,8,24,18,20,28,14},{23,7,27,1,5,3,11,17,13,31..., dimensions={0} | all-to-all | bytes 524288 | tf_op jit(solution)/shard_map/all_to_all | solution.py:212
  34.1 0.3 gram_term.1.refs_0_
  34.5 0.0 collective-permute-start.2
  34.5 0.8 %filtered_block.1.refs_2_ = bf16[1,64,128]{2,1,0:T(8,128)(2,1)} custom-call(bf16[16,64,128]{2,1,0:T(8,128)(2,1)S(1)} %all_to_all.16.parts_ref), custom_call_target="tpu_custom_call" | custom-call | bytes 262144 | tf_op jit(solution)/shard_map/filtered_block/pallas_call | solution.py:166
  35.3 0.4 collective-permute-done.2.refs_1_
  35.7 9.7 %all_to_all.17.terms_ref = bf16[16,32,128]{2,1,0:T(8,128)(2,1)S(1)} all-to-all(bf16[16,32,128]{2,1,0:T(8,128)(2,1)S(1)} %chip_terms.1), channel_id=1, replica_groups={{22,6,26,0,4,2,10,16,12,30,8,24,18,20,28,14},{23,7,27,1,5,3,11,17,13,31..., dimensions={0} | all-to-all | bytes 262144 | tf_op jit(solution)/shard_map/all_to_all | solution.py:212
  45.4 0.7 %gram_sum.1 = f32[64,64]{1,0:T(8,128)} custom-call(bf16[16,32,128]{2,1,0:T(8,128)(2,1)S(1)} %all_to_all.17.terms_ref), custom_call_target="tpu_custom_call" | custom-call | bytes 131072 | tf_op jit(solution)/shard_map/gram_sum/pallas_call | solution.py:187
  (2 shorter events, 0.1 us)
Async XLA Ops:
  0.6 2.0 %copy-start = (bf16[1,1,96,128,128]{4,3,2,1,0:T(8,128)(2,1)S(1)}, bf16[1,1,96,128,128]{4,3,2,1,0:T(8,128)(2,1)}, u32[]{:S(2)}) copy-start(bf16[1,1,96,128,128]{4,3,2,1,0:T(8,128)(2,1)} %param.6) | copy-start | bytes 9437188
  0.6 2.0 %copy-start.1 = (bf16[1,128,64]{1,2,0:T(8,128)(2,1)S(1)}, bf16[1,128,64]{1,2,0:T(8,128)(2,1)}, u32[]{:S(2)}) copy-start(bf16[1,128,64]{1,2,0:T(8,128)(2,1)} %param.5) | copy-start | bytes 49156
  0.7 2.0 %collective-permute-start = (bf16[1,64,128]{2,1,0:T(8,128)(2,1)}, bf16[1,64,128]{2,1,0:T(8,128)(2,1)S(1)}, u32[]{:S(2)}, u32[]{:S(2)}) collective-permute-start(bf16[1,64,128]{2,1,0:T(8,128)(2,1)} %bitcast.5), channel_id=1, source_target_pairs={{0,1},{1,0},{2,3},{3,2},{4,5},{5,4},{6,7},{7,6},{8,9},{9,8},{10,11... | collective-permute-start | bytes 49160 | tf_op jit(solution)/shard_map/ppermute | solution.py:205
  19.2 1.2 %collective-permute-start.1 = (bf16[1,64,128]{2,1,0:T(8,128)(2,1)S(1)}, bf16[1,64,128]{2,1,0:T(8,128)(2,1)S(1)}, u32[]{:S(2)}, u32[]{:S(2)}) collective-permute-start(bf16[1,64,128]{2,1,0:T(8,128)(2,1)S(1)} %sum_parts.1.refs_0_.first_ref), channel_id=1, source_target_pairs={{0,1},{1,0},{2,3},{3,2},{4,5},{5,4},{6,7},{7,6},{8,9},{9,8},{10,11... | collective-permute-start | bytes 49160 | tf_op jit(solution)/shard_map/ppermute | solution.py:205
  34.5 1.2 %collective-permute-start.2 = (f32[1,32,128]{2,1,0:T(8,128)S(1)}, f32[1,32,128]{2,1,0:T(8,128)S(1)}, u32[]{:S(2)}, u32[]{:S(2)}) collective-permute-start(f32[1,32,128]{2,1,0:T(8,128)S(1)} %gram_term.1.refs_0_), channel_id=1, source_target_pairs={{0,1},{1,0},{2,3},{3,2},{4,5},{5,4},{6,7},{7,6},{8,9},{9,8},{10,11... | collective-permute-start | bytes 49160 | tf_op jit(solution)/shard_map/ppermute | solution.py:205

commit v8 on v7

--- a/solution.py
+++ b/solution.py
@@ -208,7 +208,7 @@
     lead = n_col * 3 // 4 - 1
     order = MEASURED_ORDER.get(n_col, sorted(range(n_col), key=lambda k: k ^ lead))
 
-    def scatter(blocks):
+    def scatter(blocks, order=order):
         return lax.all_to_all(blocks, "col", 0, 0, tiled=True, axis_index_groups=[order])
 
     x_turned = jnp.swapaxes(x_block, 1, 2)
@@ -221,7 +221,8 @@
     parts = scatter(partial)
     terms = exchange(gram_term(parts, first))
     filtered = filtered_block(parts)
-    terms = scatter(chip_terms(terms, filtered, n_col))
+    gram_order = sorted(range(n_col), key=lambda k: k ^ lead)
+    terms = scatter(chip_terms(terms, filtered, n_col), gram_order)
     return jnp.swapaxes(filtered, 1, 2), gram_sum(terms, 1.0 / (n_col * n_row * 128))
 
 

time: 46.4 us -> 46.3 us (level)
  no operation moved by 1% of the time
where the time goes in v8:
time: 46.3 us; the launch traced here: 46.1 us
  blocking collectives  37.4 us (81%)
  Pallas kernels  5.1 us (11%)
  waiting for transfers between devices  1.58 us (3%)
  between operations  1.37 us (3%)
  starting transfers between devices  0.62 us (1%)
    all_to_all x3, blocking collectives, scatter(): lax.all_to_all(blocks, 'col', 0, 0, tiled=True, axis_index_groups=[order])  37.4 us
    pallas_call x2, Pallas kernels, tile_products(): call(functools.partial(products_kernel, order, own_first, transposed), ja...  2.43 us
    ppermute x3, waiting for transfers between devices, exchange(): return (vecs, lax.ppermute(vecs, 'row', [(0, 1), (1, 0)]))  1.58 us
  transfers between devices with their start and end apart: 3, of which 2 were waited for; matrix products, arithmetic and copies ran while one was open for 0% of the time, Pallas kernels for 3%

profile of v8, /device:TPU:0, one launch (start us, length us, event | category | flops | bytes accessed | tf_op | source)
XLA Modules:
  0.0 46.1 jit_solution(12513696705000873055)
XLA Ops:
  0.6 0.0 copy-start
  0.6 0.0 copy-start.1
  0.7 0.5 %collective-permute-start = (bf16[1,64,128]{2,1,0:T(8,128)(2,1)}, bf16[1,64,128]{2,1,0:T(8,128)(2,1)S(1)}, u32[]{:S(2)}, u32[]{:S(2)}) collective-permute-start(bf16[1,64,128]{2,1,0:T(8,128)(2,1)} %bitcast.5), channel_id=1, source_target_pairs={{0,1},{1,0},{2,3},{3,2},{4,5},{5,4},{6,7},{7,6},{8,9},{9,8},{10,11... | collective-permute-start | bytes 49160 | tf_op jit(solution)/shard_map/ppermute | solution.py:205
  1.2 0.8 %stage.1 = (s32[1,1,96]{2,1,0:T(1,128)S(4)}, s32[1,1,96]{2,1,0:T(1,128)S(4)}) custom-call(s32[1,1,96]{2,1,0:T(1,128)} %rows_ref.1, s32[1,1,96]{2,1,0:T(1,128)} %cols_ref.1), custom_call_target="tpu_custom_call" | custom-call | flops 3000000000 | tf_op jit(solution)/shard_map/stage/pallas_call | solution.py:65
  2.7 0.0 collective-permute-done.refs_1_
  2.7 0.0 copy-done
  2.7 0.0 copy-done.1
  2.7 1.2 %tile_products.2 = bf16[16,64,128]{2,1,0:T(8,128)(2,1)S(1)} custom-call(s32[1,1,96]{2,1,0:T(1,128)S(4)} %get-tuple-element.4.rows, s32[1,1,96]{2,1,0:T(1,128)S(4)} %get-tuple-element.5.cols, s32[1,1]{1,0:T(1,128)S(6)} %copy.7.count_ref, bf16[96,128,128]{2,1,0:T(8,128)(2,1)S(1)} %bitcast.3, bf16[1,64,128]{2,1,0:T(8,128)(2,1)S(1)} %bitcast.6, ...), custom_call_target="tpu_custom_call" | custom-call | flops 805306368 | bytes 3145728 | tf_op jit(solution)/shard_map/tile_products/pallas_call | solution.py:120
  3.9 15.2 %all_to_all.15.parts_ref = bf16[16,64,128]{2,1,0:T(8,128)(2,1)S(1)} all-to-all(bf16[16,64,128]{2,1,0:T(8,128)(2,1)S(1)} %tile_products.2), channel_id=1, replica_groups={{22,6,26,0,4,2,10,16,12,30,8,24,18,20,28,14},{23,7,27,1,5,3,11,17,13,31..., dimensions={0} | all-to-all | bytes 524288 | tf_op jit(solution)/shard_map/all_to_all | solution.py:212
  19.2 0.1 collective-permute-start.1
  19.3 1.2 %collective-permute-done.1.refs_1_ = bf16[1,64,128]{2,1,0:T(8,128)(2,1)S(1)} collective-permute-done((bf16[1,64,128]{2,1,0:T(8,128)(2,1)S(1)}, bf16[1,64,128]{2,1,0:T(8,128)(2,1)S(1)}, u32[]{:S(2)}, u32[]{:S(2)}) %collective-permute-start.1) | collective-permute-done | bytes 16416 | tf_op jit(solution)/shard_map/ppermute | solution.py:205
  20.4 1.2 %tile_products.3 = bf16[16,64,128]{2,1,0:T(8,128)(2,1)S(1)} custom-call(s32[1,1,96]{2,1,0:T(1,128)S(4)} %get-tuple-element.4.rows, s32[1,1,96]{2,1,0:T(1,128)S(4)} %get-tuple-element.5.cols, s32[1,1]{1,0:T(1,128)S(6)} %copy.7.count_ref, bf16[96,128,128]{2,1,0:T(8,128)(2,1)S(1)} %bitcast.4, bf16[1,64,128]{2,1,0:T(8,128)(2,1)S(1)} %sum_parts.1.refs_0_.first_ref, ...), custom_call_target="tpu_custom_call" | custom-call | flops 805306368 | bytes 3145728 | tf_op jit(solution)/shard_map/tile_products/pallas_call | solution.py:120
  21.6 12.5 %all_to_all.16.parts_ref = bf16[16,64,128]{2,1,0:T(8,128)(2,1)S(1)} all-to-all(bf16[16,64,128]{2,1,0:T(8,128)(2,1)S(1)} %tile_products.3), channel_id=1, replica_groups={{22,6,26,0,4,2,10,16,12,30,8,24,18,20,28,14},{23,7,27,1,5,3,11,17,13,31..., dimensions={0} | all-to-all | bytes 524288 | tf_op jit(solution)/shard_map/all_to_all | solution.py:212
  34.1 0.3 gram_term.1.refs_0_
  34.4 0.0 collective-permute-start.2
  34.5 0.8 %filtered_block.1.refs_2_ = bf16[1,64,128]{2,1,0:T(8,128)(2,1)} custom-call(bf16[16,64,128]{2,1,0:T(8,128)(2,1)S(1)} %all_to_all.16.parts_ref), custom_call_target="tpu_custom_call" | custom-call | bytes 262144 | tf_op jit(solution)/shard_map/filtered_block/pallas_call | solution.py:166
  35.3 0.4 collective-permute-done.2.refs_1_
  35.7 9.7 %all_to_all.17.terms_ref = bf16[16,32,128]{2,1,0:T(8,128)(2,1)S(1)} all-to-all(bf16[16,32,128]{2,1,0:T(8,128)(2,1)S(1)} %chip_terms.1), channel_id=1, replica_groups={{22,20,18,16,30,28,26,24,6,4,2,0,14,12,10,8},{23,21,19,17,31,29,27,25,7..., dimensions={0} | all-to-all | bytes 262144 | tf_op jit(solution)/shard_map/all_to_all | solution.py:212
  45.4 0.7 %gram_sum.1 = f32[64,64]{1,0:T(8,128)} custom-call(bf16[16,32,128]{2,1,0:T(8,128)(2,1)S(1)} %all_to_all.17.terms_ref), custom_call_target="tpu_custom_call" | custom-call | bytes 131072 | tf_op jit(solution)/shard_map/gram_sum/pallas_call | solution.py:187
  (2 shorter events, 0.1 us)
Async XLA Ops:
  0.6 2.0 %copy-start = (bf16[1,1,96,128,128]{4,3,2,1,0:T(8,128)(2,1)S(1)}, bf16[1,1,96,128,128]{4,3,2,1,0:T(8,128)(2,1)}, u32[]{:S(2)}) copy-start(bf16[1,1,96,128,128]{4,3,2,1,0:T(8,128)(2,1)} %param.6) | copy-start | bytes 9437188
  0.6 2.0 %copy-start.1 = (bf16[1,128,64]{1,2,0:T(8,128)(2,1)S(1)}, bf16[1,128,64]{1,2,0:T(8,128)(2,1)}, u32[]{:S(2)}) copy-start(bf16[1,128,64]{1,2,0:T(8,128)(2,1)} %param.5) | copy-start | bytes 49156
  0.7 2.0 %collective-permute-start = (bf16[1,64,128]{2,1,0:T(8,128)(2,1)}, bf16[1,64,128]{2,1,0:T(8,128)(2,1)S(1)}, u32[]{:S(2)}, u32[]{:S(2)}) collective-permute-start(bf16[1,64,128]{2,1,0:T(8,128)(2,1)} %bitcast.5), channel_id=1, source_target_pairs={{0,1},{1,0},{2,3},{3,2},{4,5},{5,4},{6,7},{7,6},{8,9},{9,8},{10,11... | collective-permute-start | bytes 49160 | tf_op jit(solution)/shard_map/ppermute | solution.py:205
  19.2 1.2 %collective-permute-start.1 = (bf16[1,64,128]{2,1,0:T(8,128)(2,1)S(1)}, bf16[1,64,128]{2,1,0:T(8,128)(2,1)S(1)}, u32[]{:S(2)}, u32[]{:S(2)}) collective-permute-start(bf16[1,64,128]{2,1,0:T(8,128)(2,1)S(1)} %sum_parts.1.refs_0_.first_ref), channel_id=1, source_target_pairs={{0,1},{1,0},{2,3},{3,2},{4,5},{5,4},{6,7},{7,6},{8,9},{9,8},{10,11... | collective-permute-start | bytes 49160 | tf_op jit(solution)/shard_map/ppermute | solution.py:205
  34.4 1.2 %collective-permute-start.2 = (f32[1,32,128]{2,1,0:T(8,128)S(1)}, f32[1,32,128]{2,1,0:T(8,128)S(1)}, u32[]{:S(2)}, u32[]{:S(2)}) collective-permute-start(f32[1,32,128]{2,1,0:T(8,128)S(1)} %gram_term.1.refs_0_), channel_id=1, source_target_pairs={{0,1},{1,0},{2,3},{3,2},{4,5},{5,4},{6,7},{7,6},{8,9},{9,8},{10,11... | collective-permute-start | bytes 49160 | tf_op jit(solution)/shard_map/ppermute | solution.py:205
